TPU v7x, 128 devices: a whole 4x4x4 slice. The times are simulated.
128 devices in a mesh: gx: 16 (over z, y), gy: 8 (over x, core).
Axes of the slice: x: 4, y: 4, z: 4, core: 2. Of those that a mesh axis runs over, the one named last changes fastest.
Arguments:
- adjoint_in: float32 [4, 48, 128, 1024], P(None, None, 'gx', 'gy'), may hold values from -6 to 6
- conc: float32 [4, 48, 128, 1024], P(None, None, 'gx', 'gy'), may hold values from 0 to 1
- pressure: float32 [48, 128, 1024], P(None, 'gx', 'gy'), may hold values from -3 to 3
- perm: float32 [48, 128, 1024], P(None, 'gx', 'gy'), may hold values from 0.3 to 3
- porosity: float32 [48, 128, 1024], P(None, 'gx', 'gy'), may hold values from 0.2 to 0.4
- storage: float32 [48, 128, 1024], P(None, 'gx', 'gy'), may hold values from 0.5 to 2
- rock: int32 [48, 128, 1024], P(None, 'gx', 'gy'), may hold values from 0 to 7
- upwind: int32 [4, 48, 128, 1024], P(None, None, 'gx', 'gy'), may hold values from 0 to 1, as said below
- sorption: float32 [2, 8, 4], replicated, may hold values from 0.3 to 3
Outputs:
- adjoint_out: float32 [4, 48, 128, 1024], P(None, None, 'gx', 'gy')
- grad: float32 [48, 128, 1024], P(None, 'gx', 'gy')
Inputs may be any that keep to these rules, and one draw needn't show every extreme that they name: upwind[0] and upwind[1] flag a cell's faces toward lower and higher first horizontal index, upwind[2] and upwind[3] toward lower and higher second index; a flag of 1 means the cell of lower index on that face is upwind. upwind[1] of a cell equals upwind[0] of the next cell along the first dimension, and upwind[3] equals upwind[2] of the next cell along the second. Flags on the outer boundary of the grid are arbitrary.
All inputs are finite; a program needn't handle non-finite values.
Results may differ from a plain program's by a relative error of at most 0.0003.
Values sent between devices are 32-bit elements; how exact they have to be, the bound alone decides.
A program may use at most 256 MiB of HBM per device.

v0:
```python
import jax
import jax.numpy as jnp
from jax import lax
from jax.experimental import pallas as pl
from jax.experimental.pallas import tpu as pltpu
from jax.sharding import PartitionSpec as P

ROCKS = 8
SUB = 8
CHEB = 4
SPEC = 4
NZ = 48
BX = 8
LANES = 128
ZT = NZ // 8
STEP = 0.02
CONTRACT = 0.9
F32 = jnp.float32
MESH = pl.DeviceIdType.MESH

CHEB_SLOT = SUB * SPEC
PERM_SLOT = CHEB_SLOT + CHEB
PRESS_SLOT = PERM_SLOT + 1
CONC_SLOT = PERM_SLOT + 2
SLOTS = PERM_SLOT + 3


def iota(shape, dim):
    return lax.broadcasted_iota(jnp.int32, shape, dim)


def pack_row(values, x, packed):
    pair = iota((8, LANES), 1) // 2
    for zt in range(ZT):
        t = x * ZT + zt
        turned = pltpu.roll(values[8 * zt:8 * zt + 8], 2 * t + 1, 1)
        packed = jnp.where(pair == t, turned, packed)
    return packed


def unpack_row(packed, x):
    tiles = []
    for zt in range(ZT):
        t = x * ZT + zt
        tiles.append(pltpu.roll(packed, LANES - 2 * t, 1) if t else packed)
    return jnp.concatenate(tiles, axis=0)


def align(left, right):
    even = iota((8, LANES), 1) % 2 == 0
    return jnp.where(even, left, pltpu.roll(right, LANES - 2, 1))


def kernel(adj_h, conc_h, press_h, perm_h, por_h, sto_h, rock_h, up_h, sorp, out_h, grad_h,
           adj, conc, press, perm, por, sto, rock, up, ia, w, wacc, py, hyl, hyr, hyw, pw,
           ps, psl, psr, coef, tau, st, kk, d, dpy, dhl, dhr, m, r, grad, in_sems, send, recv):
    gx = lax.axis_index("gx")
    gy = lax.axis_index("gy")
    nx = lax.axis_size("gx")
    ny = lax.axis_size("gy")
    to = [
        {"gx": lax.rem(gx + nx - 1, nx), "gy": gy},
        {"gx": lax.rem(gx + 1, nx), "gy": gy},
        {"gx": gx, "gy": lax.rem(gy + ny - 1, ny)},
        {"gx": gx, "gy": lax.rem(gy + 1, ny)},
    ]

    loads = {}

    def load(i, name, src, dst):
        loads[name] = []
        for x in range(BX):
            copy = pltpu.make_async_copy(src(x), dst(x), in_sems.at[i, x])
            copy.start()
            loads[name].append(copy)

    def arrived(*names):
        for name in names:
            for copy in loads[name]:
                copy.wait()

    barrier = pltpu.get_barrier_semaphore()
    for target in to:
        pl.semaphore_signal(barrier, inc=1, device_id=target, device_id_type=MESH)
    load(0, "conc", lambda x: conc_h.at[:, :, x, :], lambda x: conc.at[x + 1])
    load(1, "rock", lambda x: rock_h.at[:, x, :], lambda x: rock.at[x])
    load(2, "por", lambda x: por_h.at[:, x, :], lambda x: por.at[x])
    load(3, "adj", lambda x: adj_h.at[:, :, x, :], lambda x: adj.at[x])
    load(4, "perm", lambda x: perm_h.at[:, x, :], lambda x: perm.at[x + 1])
    load(5, "press", lambda x: press_h.at[:, x, :], lambda x: press.at[x + 1])
    load(6, "up", lambda x: up_h.at[:, :, x, :], lambda x: up.at[x])
    load(7, "sto", lambda x: sto_h.at[:, x, :], lambda x: sto.at[x])

    def message(slot, way, src, dst):
        return pltpu.make_async_remote_copy(
            src_ref=src, dst_ref=dst, send_sem=send.at[slot, way], recv_sem=recv.at[slot, way],
            device_id=to[way], device_id_type=MESH)

    def transport_messages(t, s):
        slot = t * SPEC + s
        return [
            message(slot, 0, w.at[t, 1, s], w.at[t, BX + 1, s]),
            message(slot, 1, w.at[t, BX, s], w.at[t, 0, s]),
            message(slot, 2, py.at[t, s], hyr.at[t, s]),
            message(slot, 3, py.at[t, s], hyl.at[t, s]),
        ]

    def cheb_messages(j):
        slot = CHEB_SLOT + j
        return [
            message(slot, 0, d.at[j, 1], d.at[j, BX + 1]),
            message(slot, 1, d.at[j, BX], d.at[j, 0]),
            message(slot, 2, dpy.at[j], dhr.at[j]),
            message(slot, 3, dpy.at[j], dhl.at[j]),
        ]

    setup = [
        message(PERM_SLOT, 0, perm.at[1], perm.at[BX + 1]),
        message(PERM_SLOT, 1, perm.at[BX], perm.at[0]),
        message(PRESS_SLOT, 0, press.at[1], press.at[BX + 1]),
        message(PRESS_SLOT, 1, press.at[BX], press.at[0]),
        message(PERM_SLOT, 2, ps, psr),
        message(PERM_SLOT, 3, ps, psl),
        message(CONC_SLOT, 0, conc.at[1], conc.at[BX + 1]),
        message(CONC_SLOT, 1, conc.at[BX], conc.at[0]),
    ]

    zero_tile = jnp.zeros((8, LANES), F32)
    lane = iota((NZ, LANES), 1)
    first_lane = lane == 0
    last_lane = lane == LANES - 1
    level = iota((NZ, LANES), 0)

    arrived("conc", "rock", "por", "adj")
    for x in range(BX):
        kind = rock[x]
        bits = [(kind // (1 << b)) % 2 == 1 for b in range(3)]

        def look_up(row, s):
            level_values = [sorp[row, i, s] for i in range(ROCKS)]
            for b in range(3):
                level_values = [
                    jnp.where(bits[b], level_values[2 * i + 1], level_values[2 * i])
                    for i in range(len(level_values) // 2)
                ]
            return level_values[0]

        hole = por[x]
        for s in range(SPEC):
            lang = look_up(0, s)
            cap = look_up(1, s)
            base = 1.0 + lang * conc[x + 1, s]
            base = base * base
            inv = base / (hole * (base + cap * lang))
            ia[x, s] = inv
            first = adj[x, s] * inv
            w[0, x + 1, s] = first
            wacc[x + 1, s] = first
    for s in range(SPEC):
        packed = zero_tile
        for x in range(BX):
            packed = pack_row(w[0, x + 1, s], x, packed)
        py[0, s] = packed
        pw[s] = packed
    arrived("perm", "press")
    for i, field in enumerate((perm, press)):
        packed = zero_tile
        for x in range(BX):
            packed = pack_row(field[x + 1], x, packed)
        ps[i] = packed
    for s in range(SPEC):
        packed = zero_tile
        for x in range(BX):
            packed = pack_row(conc[x + 1, s], x, packed)
        ps[2 + s] = packed

    pl.semaphore_wait(barrier, 4)
    for copy in setup[:6]:
        copy.start()
    for s in range(SPEC):
        for copy in transport_messages(0, s):
            copy.start()
    for copy in setup[6:]:
        copy.start()

    arrived("up", "sto")
    for copy in setup[:6]:
        copy.wait_recv()
    even = iota((8, LANES), 1) % 2 == 0
    perm_edge = align(psl[0], psr[0])
    perm_edge = jnp.where(even, jnp.where(gy == 0, 0.0, perm_edge), jnp.where(gy == ny - 1, 0.0, perm_edge))
    press_edge = align(psl[1], psr[1])
    for x in range(BX):
        own = perm[x + 1]
        head = press[x + 1]
        perm_n = perm[x] if x > 0 else jnp.where(gx == 0, 0.0, perm[x])
        perm_s = perm[x + 2] if x < BX - 1 else jnp.where(gx == nx - 1, 0.0, perm[x + 2])
        edge = unpack_row(perm_edge, x)
        perm_w = jnp.where(first_lane, edge, pltpu.roll(own, 1, 1))
        perm_e = jnp.where(last_lane, edge, pltpu.roll(own, LANES - 1, 1))
        perm_b = jnp.where(level == 0, 0.0, pltpu.roll(own, 1, 0))
        perm_a = jnp.where(level == NZ - 1, 0.0, pltpu.roll(own, NZ - 1, 0))
        edge = unpack_row(press_edge, x)
        drops = [
            head - press[x],
            head - press[x + 2],
            head - jnp.where(first_lane, edge, pltpu.roll(head, 1, 1)),
            head - jnp.where(last_lane, edge, pltpu.roll(head, LANES - 1, 1)),
            head - pltpu.roll(head, 1, 0),
            head - pltpu.roll(head, NZ - 1, 0),
        ]
        trans = []
        for i, near in enumerate((perm_n, perm_s, perm_w, perm_e, perm_b, perm_a)):
            inv = 1.0 / (own + near)
            trans.append(2.0 * own * near * inv)
            share = near * inv
            kk[i, x] = 2.0 * share * share * drops[i]
        total = sto[x]
        for item in trans:
            total = total + item
        inv_diag = 1.0 / total
        centre = None
        for i in range(4):
            up_here = (up[x, i] == 1) if i in (1, 3) else (up[x, i] != 1)
            push = jnp.where(up_here, STEP * trans[i] * jnp.abs(drops[i]), 0.0)
            coef[i, x] = push
            centre = push if centre is None else centre + push
        coef[4, x] = centre
        for i in range(6):
            ratio = trans[i] * inv_diag
            tau[i, x] = ratio
            if i < 4:
                ratio = STEP * ratio
                st[i, x] = jnp.where(drops[i] > 0, ratio, jnp.where(drops[i] < 0, -ratio, 0.0))

    def advance(t, s, last):
        for copy in transport_messages(t, s):
            copy.wait_recv()
        halo = align(hyl[t, s], hyr[t, s])

        @pl.when(t == 0)
        def _():
            hyw[s] = halo
            wacc[0, s] = w[t, 0, s]
            wacc[BX + 1, s] = w[t, BX + 1, s]

        @pl.when(t > 0)
        def _():
            hyw[s] = hyw[s] + halo
            wacc[0, s] = wacc[0, s] + w[t, 0, s]
            wacc[BX + 1, s] = wacc[BX + 1, s] + w[t, BX + 1, s]

        packed = zero_tile
        for x in range(BX):
            value = w[t, x + 1, s]
            edge = unpack_row(halo, x)
            west = jnp.where(first_lane, edge, pltpu.roll(value, 1, 1))
            east = jnp.where(last_lane, edge, pltpu.roll(value, LANES - 1, 1))
            moved = (
                adj[x, s]
                + (coef[0, x] * w[t, x, s] + coef[1, x] * w[t, x + 2, s])
                + (coef[2, x] * west + coef[3, x] * east)
                - coef[4, x] * value
            )
            adj[x, s] = moved
            if not last:
                after = moved * ia[x, s]
                w[t + 1, x + 1, s] = after
                wacc[x + 1, s] = wacc[x + 1, s] + after
                packed = pack_row(after, x, packed)
        if not last:
            py[t + 1, s] = packed
            pw[s] = pw[s] + packed
            for copy in transport_messages(t + 1, s):
                copy.start()

    @pl.loop(0, (SUB - 1) * SPEC)
    def _(i):
        advance(i // SPEC, i % SPEC, False)

    @pl.loop(0, SPEC)
    def _(s):
        advance(SUB - 1, s, True)

    writes = []
    for x in range(BX):
        copy = pltpu.make_async_copy(adj.at[x], out_h.at[:, :, x, :], in_sems.at[0, x])
        copy.start()
        writes.append(copy)

    for copy in setup[6:]:
        copy.wait_recv()
    flag_edge = zero_tile
    for x in range(BX):
        flag_edge = pack_row(jnp.where(first_lane, up[x, 2], up[x, 3]).astype(F32), x, flag_edge)
    flag_edge = pltpu.roll(flag_edge, LANES - 1, 1) == 1.0
    face_edge = zero_tile
    for s in range(SPEC):
        sum_halo = hyw[s]
        sum_own = pltpu.roll(pw[s], LANES - 1, 1)
        conc_halo = align(psl[2 + s], psr[2 + s])
        conc_own = pltpu.roll(ps[2 + s], LANES - 1, 1)
        low = jnp.where(even, conc_halo, conc_own)
        high = jnp.where(even, conc_own, conc_halo)
        rise = jnp.where(even, sum_own - sum_halo, sum_halo - sum_own)
        face_edge = face_edge + jnp.where(flag_edge, low, high) * rise

    def x_face(x):
        flag = (up[x, 0] if x < BX else up[x - 1, 1]) == 1
        total = None
        for s in range(SPEC):
            term = jnp.where(flag, conc[x, s], conc[x + 1, s]) * (wacc[x + 1, s] - wacc[x, s])
            total = term if total is None else total + term
        return total

    before = x_face(0)
    packed = zero_tile
    for x in range(BX):
        after = x_face(x + 1)
        flag = up[x, 3] == 1
        east = None
        for s in range(SPEC):
            here = conc[x + 1, s]
            mine = wacc[x + 1, s]
            term = jnp.where(flag, here, pltpu.roll(here, LANES - 1, 1)) * (pltpu.roll(mine, LANES - 1, 1) - mine)
            east = term if east is None else east + term
        edge = unpack_row(face_edge, x)
        west = jnp.where(first_lane, edge, pltpu.roll(east, 1, 1))
        east = jnp.where(last_lane, edge, east)
        faces = (before, after, west, east)
        start = None
        slope = None
        for i in range(4):
            one = st[i, x] * faces[i]
            two = jnp.abs(kk[i, x]) * faces[i]
            start = one if start is None else start + one
            slope = two if slope is None else slope + two
        grad[x] = STEP * slope
        d[0, x + 1] = start
        r[x] = start
        m[x] = start
        packed = pack_row(start, x, packed)
        before = after
    dpy[0] = packed
    for copy in cheb_messages(0):
        copy.start()

    def neighbours(j, x, halo):
        value = d[j, x + 1]
        edge = unpack_row(halo, x)
        return (
            d[j, x],
            d[j, x + 2],
            jnp.where(first_lane, edge, pltpu.roll(value, 1, 1)),
            jnp.where(last_lane, edge, pltpu.roll(value, LANES - 1, 1)),
            pltpu.roll(value, 1, 0),
            pltpu.roll(value, NZ - 1, 0),
        )

    rho = CONTRACT
    for j in range(CHEB - 1):
        rho_next = 1.0 / (2.0 / CONTRACT - rho)
        for copy in cheb_messages(j):
            copy.wait_recv()
        halo = align(dhl[j], dhr[j])
        packed = zero_tile
        for x in range(BX):
            value = d[j, x + 1]
            residue = r[x] - value
            for i, near in enumerate(neighbours(j, x, halo)):
                residue = residue + tau[i, x] * near
            r[x] = residue
            value = (rho_next * rho) * value + (2.0 * rho_next / CONTRACT) * residue
            total = m[x] + value
            m[x] = total
            if j == CHEB - 2:
                value = total
            d[j + 1, x + 1] = value
            packed = pack_row(value, x, packed)
        dpy[j + 1] = packed
        for copy in cheb_messages(j + 1):
            copy.start()
        rho = rho_next

    j = CHEB - 1
    for copy in cheb_messages(j):
        copy.wait_recv()
    halo = align(dhl[j], dhr[j])
    for x in range(BX):
        value = d[j, x + 1]
        total = grad[x]
        for i, near in enumerate(neighbours(j, x, halo)):
            total = total - kk[i, x] * (value - near)
        grad[x] = total
        copy = pltpu.make_async_copy(grad.at[x], grad_h.at[:, x, :], in_sems.at[1, x])
        copy.start()
        writes.append(copy)

    for copy in setup:
        copy.wait_send()
    for j in range(CHEB):
        for copy in cheb_messages(j):
            copy.wait_send()

    @pl.loop(0, SUB * SPEC)
    def _(i):
        for copy in transport_messages(i // SPEC, i % SPEC):
            copy.wait_send()

    for copy in writes:
        copy.wait()


def body(adjoint_in, conc, pressure, perm, porosity, storage, rock, upwind, sorption):
    def vmem(*shape, dtype=F32):
        return pltpu.VMEM(shape, dtype)

    row = (NZ, LANES)
    tile = (8, LANES)
    hbm = pl.BlockSpec(memory_space=pl.ANY)
    return tuple(pl.pallas_call(
        kernel,
        out_shape=(
            jax.ShapeDtypeStruct(adjoint_in.shape, F32),
            jax.ShapeDtypeStruct(pressure.shape, F32),
        ),
        in_specs=[hbm] * 8 + [pl.BlockSpec(memory_space=pltpu.SMEM)],
        out_specs=(hbm, hbm),
        scratch_shapes=[
            vmem(BX, SPEC, *row),
            vmem(BX + 2, SPEC, *row),
            vmem(BX + 2, *row),
            vmem(BX + 2, *row),
            vmem(BX, *row),
            vmem(BX, *row),
            vmem(BX, *row, dtype=jnp.int32),
            vmem(BX, 4, *row, dtype=jnp.int32),
            vmem(BX, SPEC, *row),
            vmem(SUB, BX + 2, SPEC, *row),
            vmem(BX + 2, SPEC, *row),
            vmem(SUB, SPEC, *tile),
            vmem(SUB, SPEC, *tile),
            vmem(SUB, SPEC, *tile),
            vmem(SPEC, *tile),
            vmem(SPEC, *tile),
            vmem(2 + SPEC, *tile),
            vmem(2 + SPEC, *tile),
            vmem(2 + SPEC, *tile),
            vmem(5, BX, *row),
            vmem(6, BX, *row),
            vmem(4, BX, *row),
            vmem(6, BX, *row),
            vmem(CHEB, BX + 2, *row),
            vmem(CHEB, *tile),
            vmem(CHEB, *tile),
            vmem(CHEB, *tile),
            vmem(BX, *row),
            vmem(BX, *row),
            vmem(BX, *row),
            pltpu.SemaphoreType.DMA((8, BX)),
            pltpu.SemaphoreType.DMA((SLOTS, 4)),
            pltpu.SemaphoreType.DMA((SLOTS, 4)),
        ],
        compiler_params=pltpu.CompilerParams(
            collective_id=0, has_side_effects=True, vmem_limit_bytes=48 * 2**20),
    )(adjoint_in, conc, pressure, perm, porosity, storage, rock, upwind, sorption))


def solution(mesh):
    in_specs = (
        P(None, None, "gx", "gy"),
        P(None, None, "gx", "gy"),
        P(None, "gx", "gy"),
        P(None, "gx", "gy"),
        P(None, "gx", "gy"),
        P(None, "gx", "gy"),
        P(None, "gx", "gy"),
        P(None, None, "gx", "gy"),
        P(),
    )
    out_specs = (P(None, None, "gx", "gy"), P(None, "gx", "gy"))
    return jax.shard_map(body, mesh=mesh, in_specs=in_specs, out_specs=out_specs, check_vma=False)
```

profile of v0, /device:TPU:1, one launch (start us, length us, event | category | flops | bytes accessed | tf_op | source)
XLA Modules:
  0.0 88.4 jit_solution(1275825164806502837)
XLA Ops:
  0.6 0.8 copy.11.sorp
  1.4 0.0 copy-start
  1.4 1.1 %copy-done = f32[4,48,8,128]{3,2,1,0:T(8,128)S(1)} copy-done((f32[4,48,8,128]{3,2,1,0:T(8,128)S(1)}, f32[4,48,8,128]{3,2,1,0:T(8,128)}, u32[]{:S(2)}) %copy-start) | copy-done | bytes 786456
  2.5 0.0 copy-start.1
  2.5 1.1 %copy-done.1 = f32[4,48,8,128]{3,2,1,0:T(8,128)S(1)} copy-done((f32[4,48,8,128]{3,2,1,0:T(8,128)S(1)}, f32[4,48,8,128]{3,2,1,0:T(8,128)}, u32[]{:S(2)}) %copy-start.1) | copy-done | bytes 786456
  3.7 0.0 copy-start.2
  3.7 1.1 %copy-done.2 = s32[4,48,8,128]{3,2,1,0:T(8,128)S(1)} copy-done((s32[4,48,8,128]{3,2,1,0:T(8,128)S(1)}, s32[4,48,8,128]{3,2,1,0:T(8,128)}, u32[]{:S(2)}) %copy-start.2) | copy-done | bytes 786456
  4.8 0.0 copy-start.3
  4.8 0.9 %copy-done.3 = f32[48,8,128]{2,1,0:T(8,128)S(1)} copy-done((f32[48,8,128]{2,1,0:T(8,128)S(1)}, f32[48,8,128]{2,1,0:T(8,128)}, u32[]{:S(2)}) %copy-start.3) | copy-done | bytes 196632
  5.7 0.0 copy-start.4
  5.7 0.9 %copy-done.4 = f32[48,8,128]{2,1,0:T(8,128)S(1)} copy-done((f32[48,8,128]{2,1,0:T(8,128)S(1)}, f32[48,8,128]{2,1,0:T(8,128)}, u32[]{:S(2)}) %copy-start.4) | copy-done | bytes 196632
  6.7 0.0 copy-start.5
  6.7 0.9 %copy-done.5 = f32[48,8,128]{2,1,0:T(8,128)S(1)} copy-done((f32[48,8,128]{2,1,0:T(8,128)S(1)}, f32[48,8,128]{2,1,0:T(8,128)}, u32[]{:S(2)}) %copy-start.5) | copy-done | bytes 196632
  7.6 0.0 copy-start.6
  7.6 0.9 %copy-done.6 = f32[48,8,128]{2,1,0:T(8,128)S(1)} copy-done((f32[48,8,128]{2,1,0:T(8,128)S(1)}, f32[48,8,128]{2,1,0:T(8,128)}, u32[]{:S(2)}) %copy-start.6) | copy-done | bytes 196632
  8.5 0.0 copy-start.7
  8.5 0.9 %copy-done.7 = s32[48,8,128]{2,1,0:T(8,128)S(1)} copy-done((s32[48,8,128]{2,1,0:T(8,128)S(1)}, s32[48,8,128]{2,1,0:T(8,128)}, u32[]{:S(2)}) %copy-start.7) | copy-done | bytes 196632
  9.4 77.4 %shard_map.104 = (f32[4,48,8,128]{3,2,1,0:T(8,128)S(1)}, f32[48,8,128]{2,1,0:T(8,128)S(1)}) custom-call(f32[4,48,8,128]{3,2,1,0:T(8,128)S(1)} %copy-done, f32[4,48,8,128]{3,2,1,0:T(8,128)S(1)} %copy-done.1, f32[48,8,128]{2,1,0:T(8,128)S(1)} %copy-done.3, f32[48,8,128]{2,1,0:T(8,128)S(1)} %copy-done.4, f32[48,8,128]{2,1,0:T(8,128)S(1)} %copy-done.5, ...), custom_call_target="tpu_custom_call" | custom-call | tf_op jit(solution)/shard_map/pallas_call | solution.py:421
  86.8 0.9 copy.14
  87.7 0.7 copy.15
Async XLA Ops:
  1.4 1.1 %copy-start = (f32[4,48,8,128]{3,2,1,0:T(8,128)S(1)}, f32[4,48,8,128]{3,2,1,0:T(8,128)}, u32[]{:S(2)}) copy-start(f32[4,48,8,128]{3,2,1,0:T(8,128)} %adj_h.1) | copy-start | bytes 2359300
  2.5 1.1 %copy-start.1 = (f32[4,48,8,128]{3,2,1,0:T(8,128)S(1)}, f32[4,48,8,128]{3,2,1,0:T(8,128)}, u32[]{:S(2)}) copy-start(f32[4,48,8,128]{3,2,1,0:T(8,128)} %conc_h.1) | copy-start | bytes 2359300
  3.7 1.1 %copy-start.2 = (s32[4,48,8,128]{3,2,1,0:T(8,128)S(1)}, s32[4,48,8,128]{3,2,1,0:T(8,128)}, u32[]{:S(2)}) copy-start(s32[4,48,8,128]{3,2,1,0:T(8,128)} %up_h.1) | copy-start | bytes 2359300
  4.8 0.9 %copy-start.3 = (f32[48,8,128]{2,1,0:T(8,128)S(1)}, f32[48,8,128]{2,1,0:T(8,128)}, u32[]{:S(2)}) copy-start(f32[48,8,128]{2,1,0:T(8,128)} %press_h.1) | copy-start | bytes 589828
  5.7 0.9 %copy-start.4 = (f32[48,8,128]{2,1,0:T(8,128)S(1)}, f32[48,8,128]{2,1,0:T(8,128)}, u32[]{:S(2)}) copy-start(f32[48,8,128]{2,1,0:T(8,128)} %perm_h.1) | copy-start | bytes 589828
  6.7 0.9 %copy-start.5 = (f32[48,8,128]{2,1,0:T(8,128)S(1)}, f32[48,8,128]{2,1,0:T(8,128)}, u32[]{:S(2)}) copy-start(f32[48,8,128]{2,1,0:T(8,128)} %por_h.1) | copy-start | bytes 589828
  7.6 0.9 %copy-start.6 = (f32[48,8,128]{2,1,0:T(8,128)S(1)}, f32[48,8,128]{2,1,0:T(8,128)}, u32[]{:S(2)}) copy-start(f32[48,8,128]{2,1,0:T(8,128)} %sto_h.1) | copy-start | bytes 589828
  8.5 0.9 %copy-start.7 = (s32[48,8,128]{2,1,0:T(8,128)S(1)}, s32[48,8,128]{2,1,0:T(8,128)}, u32[]{:S(2)}) copy-start(s32[48,8,128]{2,1,0:T(8,128)} %rock_h.1) | copy-start | bytes 589828
where the time goes:
time: 88.8 us; the launch traced here: 88.4 us
  Pallas kernels  77.4 us (87%)
  local copies, waits for them, and re-layouts  10.4 us (12%)
    pallas_call x1, Pallas kernels, body(): pl.pallas_call(kernel, out_shape=(jax.ShapeDtypeStruct(adjoint_in.shape,...  77.4 us
    unnamed x19, local copies, waits for them, and re-layouts  10.4 us

commit v1 on v0

v1 whole, which is shorter than its diff:
```python
import jax
import jax.numpy as jnp
from jax import lax
from jax.experimental import pallas as pl
from jax.experimental.pallas import tpu as pltpu
from jax.sharding import PartitionSpec as P

ROCKS = 8
SUB = 8
CHEB = 4
SPEC = 4
NZ = 48
BX = 8
LANES = 128
ZT = NZ // 8
STEP = 0.02
CONTRACT = 0.9
F32 = jnp.float32
MESH = pl.DeviceIdType.MESH

TIMES = (0, 1, 3, 5, 7)
ROUNDS = len(TIMES)

CHEB_SLOT = ROUNDS * SPEC
PERM_SLOT = CHEB_SLOT + 2
PRESS_SLOT = PERM_SLOT + 1
CONC_SLOT = PERM_SLOT + 2
COEF_SLOT = PERM_SLOT + 3
AREA_SLOT = PERM_SLOT + 4
TAU_SLOT = PERM_SLOT + 5
SLOTS = PERM_SLOT + 6


def iota(shape, dim):
    return lax.broadcasted_iota(jnp.int32, shape, dim)


def pack(rows):
    index = iota((8, LANES), 1) // 2
    packed = None
    for x, values in enumerate(rows):
        part = None
        for zt in range(ZT):
            t = x * ZT + zt
            turned = pltpu.roll(values[8 * zt:8 * zt + 8], 2 * t + 1, 1)
            part = turned if part is None else jnp.where(index >= t, turned, part)
        packed = part if packed is None else jnp.where(index >= x * ZT, part, packed)
    return packed


def pack_second(rows):
    lane = iota((8, LANES), 1)
    index = jnp.where(lane % 2 == 0, lane // 2, (lane + LANES - 3) % LANES // 2)
    packed = None
    for x, values in enumerate(rows):
        part = None
        for zt in range(ZT):
            t = x * ZT + zt
            turned = pltpu.roll(values[8 * zt:8 * zt + 8], 2 * t + 2, 1)
            part = turned if part is None else jnp.where(index >= t, turned, part)
        packed = part if packed is None else jnp.where(index >= x * ZT, part, packed)
    return packed


def unpack_row(packed, x):
    tiles = []
    for zt in range(ZT):
        t = x * ZT + zt
        tiles.append(pltpu.roll(packed, LANES - 2 * t, 1) if t else packed)
    return jnp.concatenate(tiles, axis=0)


def align(left, right):
    even = iota((8, LANES), 1) % 2 == 0
    return jnp.where(even, left, pltpu.roll(right, LANES - 2, 1))


def align_second(left, right):
    even = iota((8, LANES), 1) % 2 == 0
    return jnp.where(even, left, pltpu.roll(right, LANES - 4, 1))


def corners(north_west, north_east, south_west, south_east):
    even = iota((8, LANES), 1) % 2 == 0
    shift = 2 * ZT * (BX - 1)
    north = jnp.where(even, pltpu.roll(north_west, LANES - shift, 1), pltpu.roll(north_east, LANES - shift - 2, 1))
    south = jnp.where(even, pltpu.roll(south_west, shift, 1), pltpu.roll(south_east, shift - 2, 1))
    return north, south


def strip_sides(strip, second, own, north, south):
    lane = iota((8, LANES), 1)
    even = lane % 2 == 0
    row = 2 * ZT
    above = jnp.where((lane + 1) % LANES < row, north, pltpu.roll(strip, row, 1))
    edge = row * (BX - 1) - 1
    below = jnp.where((lane >= edge) & (lane < edge + row), south, pltpu.roll(strip, LANES - row, 1))
    return above, below, jnp.where(even, second, own), jnp.where(even, own, second)


def kernel(adj_h, conc_h, press_h, perm_h, por_h, sto_h, rock_h, up_h, sorp_h, out_h, grad_h,
           adj, conc, press, perm, por, sto, rock, up, ia, w, wacc, py, hyl, hyr, hyw,
           hc, ps, psl, psr, qs, ql, qr, ts, tl, tr, coef, tau, st, kk, d, dpy, dhl, dhr, dhc,
           m, r, grad, sorp, in_sems, send, recv):
    gx = lax.axis_index("gx")
    gy = lax.axis_index("gy")
    nx = lax.axis_size("gx")
    ny = lax.axis_size("gy")
    to = [
        {"gx": lax.rem(gx + nx - 1, nx), "gy": gy},
        {"gx": lax.rem(gx + 1, nx), "gy": gy},
        {"gx": gx, "gy": lax.rem(gy + ny - 1, ny)},
        {"gx": gx, "gy": lax.rem(gy + 1, ny)},
    ]
    to += [{"gx": a["gx"], "gy": b["gy"]} for a in to[:2] for b in to[2:]]

    loads = {}

    def load(i, name, src, dst):
        loads[name] = []
        for x in range(BX):
            copy = pltpu.make_async_copy(src(x), dst(x), in_sems.at[i, x])
            copy.start()
            loads[name].append(copy)

    def arrived(*names):
        for name in names:
            for copy in loads[name]:
                copy.wait()

    barrier = pltpu.get_barrier_semaphore()
    for target in to:
        pl.semaphore_signal(barrier, inc=1, device_id=target, device_id_type=MESH)
    table = pltpu.make_async_copy(sorp_h, sorp, in_sems.at[8, 0])
    table.start()
    load(0, "conc", lambda x: conc_h.at[:, :, x, :], lambda x: conc.at[x + 1])
    load(1, "rock", lambda x: rock_h.at[:, x, :], lambda x: rock.at[x])
    load(2, "por", lambda x: por_h.at[:, x, :], lambda x: por.at[x])
    load(3, "adj", lambda x: adj_h.at[:, :, x, :], lambda x: adj.at[x])
    load(4, "perm", lambda x: perm_h.at[:, x, :], lambda x: perm.at[x + 1])
    load(5, "press", lambda x: press_h.at[:, x, :], lambda x: press.at[x + 1])
    load(6, "up", lambda x: up_h.at[:, :, x, :], lambda x: up.at[x])
    load(7, "sto", lambda x: sto_h.at[:, x, :], lambda x: sto.at[x])

    def message(slot, way, src, dst):
        return pltpu.make_async_remote_copy(
            src_ref=src, dst_ref=dst, send_sem=send.at[slot, way], recv_sem=recv.at[slot, way],
            device_id=to[way], device_id_type=MESH)

    def row_messages(slot, field, wide):
        if wide:
            return [
                message(slot, 0, field(2, 2), field(BX + 2, 2)),
                message(slot, 1, field(BX, 2), field(0, 2)),
            ]
        return [
            message(slot, 0, field(2, 1), field(BX + 2, 1)),
            message(slot, 1, field(BX + 1, 1), field(1, 1)),
        ]

    def exchange(e, t, s, wide):
        slot = e * SPEC + s
        copies = row_messages(slot, lambda x, n: w.at[t, pl.ds(x, n), s], wide)
        if wide:
            copies += [
                message(slot, 2, py.at[e, s], hyr.at[e, s]),
                message(slot, 3, py.at[e, s], hyl.at[e, s]),
            ]
            copies += [message(slot, 4 + q, py.at[e, s, 0], hc.at[e, s, 3 - q]) for q in range(4)]
        else:
            copies += [
                message(slot, 2, py.at[e, s, 0], hyr.at[e, s, 0]),
                message(slot, 3, py.at[e, s, 0], hyl.at[e, s, 0]),
            ]
        return copies

    def cheb_exchange(e):
        slot = CHEB_SLOT + e
        copies = row_messages(slot, lambda x, n: d.at[2 * e, pl.ds(x, n)], True)
        copies += [
            message(slot, 2, dpy.at[e], dhr.at[e]),
            message(slot, 3, dpy.at[e], dhl.at[e]),
        ]
        copies += [message(slot, 4 + q, dpy.at[e, 0], dhc.at[e, 3 - q]) for q in range(4)]
        return copies

    def beside(slot, field):
        return [
            message(slot, 0, field.at[1], field.at[BX + 1]),
            message(slot, 1, field.at[BX], field.at[0]),
        ]

    second = beside(COEF_SLOT, coef) + beside(AREA_SLOT, ia) + [
        message(COEF_SLOT, 2, qs, qr),
        message(COEF_SLOT, 3, qs, ql),
    ]
    third = beside(TAU_SLOT, tau) + [
        message(TAU_SLOT, 2, ts, tr),
        message(TAU_SLOT, 3, ts, tl),
    ]
    setup = [
        message(PERM_SLOT, 0, perm.at[1], perm.at[BX + 1]),
        message(PERM_SLOT, 1, perm.at[BX], perm.at[0]),
        message(PRESS_SLOT, 0, press.at[1], press.at[BX + 1]),
        message(PRESS_SLOT, 1, press.at[BX], press.at[0]),
        message(PERM_SLOT, 2, ps, psr),
        message(PERM_SLOT, 3, ps, psl),
        message(CONC_SLOT, 0, conc.at[1], conc.at[BX + 1]),
        message(CONC_SLOT, 1, conc.at[BX], conc.at[0]),
    ]

    zero_tile = jnp.zeros((8, LANES), F32)
    lane = iota((NZ, LANES), 1)
    first_lane = lane == 0
    last_lane = lane == LANES - 1
    level = iota((NZ, LANES), 0)

    table.wait()
    arrived("conc", "rock", "por", "adj")
    for x in range(BX):
        kind = rock[x]
        bits = [(kind // (1 << b)) % 2 == 1 for b in range(3)]

        def look_up(row, s):
            level_values = [sorp[row, s, i] for i in range(ROCKS)]
            for b in range(3):
                level_values = [
                    jnp.where(bits[b], level_values[2 * i + 1], level_values[2 * i])
                    for i in range(len(level_values) // 2)
                ]
            return level_values[0]

        hole = por[x]
        for s in range(SPEC):
            lang = look_up(0, s)
            cap = look_up(1, s)
            base = 1.0 + lang * conc[x + 1, s]
            base = base * base
            inv = base / (hole * (base + cap * lang))
            ia[x + 1, s] = inv
            first = adj[x, s] * inv
            w[0, x + 2, s] = first
            wacc[x + 1, s] = first
    for s in range(SPEC):
        py[0, s, 0] = pack([w[0, x + 2, s] for x in range(BX)])
    arrived("perm", "press")
    ps[0] = pack([perm[x + 1] for x in range(BX)])
    ps[1] = pack([press[x + 1] for x in range(BX)])
    for s in range(SPEC):
        ps[2 + s] = pack([conc[x + 1, s] for x in range(BX)])

    pl.semaphore_wait(barrier, 8)
    for copy in setup[:6]:
        copy.start()
    for s in range(SPEC):
        for copy in exchange(0, 0, s, False):
            copy.start()
    for copy in setup[6:]:
        copy.start()

    arrived("up", "sto")
    for copy in setup[:6]:
        copy.wait_recv()
    even = iota((8, LANES), 1) % 2 == 0
    perm_edge = align(psl[0], psr[0])
    perm_edge = jnp.where(even, jnp.where(gy == 0, 0.0, perm_edge), jnp.where(gy == ny - 1, 0.0, perm_edge))
    press_edge = align(psl[1], psr[1])
    for x in range(BX):
        own = perm[x + 1]
        head = press[x + 1]
        perm_n = perm[x] if x > 0 else jnp.where(gx == 0, 0.0, perm[x])
        perm_s = perm[x + 2] if x < BX - 1 else jnp.where(gx == nx - 1, 0.0, perm[x + 2])
        edge = unpack_row(perm_edge, x)
        perm_w = jnp.where(first_lane, edge, pltpu.roll(own, 1, 1))
        perm_e = jnp.where(last_lane, edge, pltpu.roll(own, LANES - 1, 1))
        perm_b = jnp.where(level == 0, 0.0, pltpu.roll(own, 1, 0))
        perm_a = jnp.where(level == NZ - 1, 0.0, pltpu.roll(own, NZ - 1, 0))
        edge = unpack_row(press_edge, x)
        drops = [
            head - press[x],
            head - press[x + 2],
            head - jnp.where(first_lane, edge, pltpu.roll(head, 1, 1)),
            head - jnp.where(last_lane, edge, pltpu.roll(head, LANES - 1, 1)),
            head - pltpu.roll(head, 1, 0),
            head - pltpu.roll(head, NZ - 1, 0),
        ]
        trans = []
        for i, near in enumerate((perm_n, perm_s, perm_w, perm_e, perm_b, perm_a)):
            inv = 1.0 / (own + near)
            trans.append(2.0 * own * near * inv)
            share = near * inv
            kk[i, x] = 2.0 * share * share * drops[i]
        total = sto[x]
        for item in trans:
            total = total + item
        inv_diag = 1.0 / total
        centre = None
        for i in range(4):
            up_here = (up[x, i] == 1) if i in (1, 3) else (up[x, i] != 1)
            push = jnp.where(up_here, STEP * trans[i] * jnp.abs(drops[i]), 0.0)
            coef[x + 1, i] = push
            centre = push if centre is None else centre + push
        coef[x + 1, 4] = centre
        for i in range(6):
            ratio = trans[i] * inv_diag
            tau[x + 1, i] = ratio
            if i < 4:
                ratio = STEP * ratio
                st[i, x] = jnp.where(drops[i] > 0, ratio, jnp.where(drops[i] < 0, -ratio, 0.0))

    for i in range(4):
        qs[i] = pack([coef[x + 1, i] for x in range(BX)])
    for s in range(SPEC):
        qs[4 + s] = pack([ia[x + 1, s] for x in range(BX)])
    for copy in second:
        copy.start()

    def narrow(t, s, halo, e):
        fresh = []
        for x in range(BX):
            value = w[t, x + 2, s]
            edge = unpack_row(halo, x)
            west = jnp.where(first_lane, edge, pltpu.roll(value, 1, 1))
            east = jnp.where(last_lane, edge, pltpu.roll(value, LANES - 1, 1))
            moved = (
                adj[x, s]
                + (coef[x + 1, 0] * w[t, x + 1, s] + coef[x + 1, 1] * w[t, x + 3, s])
                + (coef[x + 1, 2] * west + coef[x + 1, 3] * east)
                - coef[x + 1, 4] * value
            )
            adj[x, s] = moved
            if e is not None:
                after = moved * ia[x + 1, s]
                w[t + 1, x + 2, s] = after
                wacc[x + 1, s] = wacc[x + 1, s] + after
                fresh.append(after)
        if e is not None:
            py[e, s, 0] = pack(fresh)
            py[e, s, 1] = pack_second(fresh)
            for copy in exchange(e, t + 1, s, True):
                copy.start()

    def wide(t, s, e):
        for copy in exchange(e, t, s, True):
            copy.wait_recv()
        strip = align(hyl[e, s, 0], hyr[e, s, 0])
        further = align_second(hyl[e, s, 1], hyr[e, s, 1])
        north, south = corners(hc[e, s, 0], hc[e, s, 1], hc[e, s, 2], hc[e, s, 3])
        sides = strip_sides(strip, further, pltpu.roll(py[e, s, 0], LANES - 1, 1), north, south)
        share = [align(ql[i], qr[i]) for i in range(4)]
        change = -(share[0] + share[1] + share[2] + share[3]) * strip
        for i in range(4):
            change = change + share[i] * sides[i]
        strip_next = strip + align(ql[4 + s], qr[4 + s]) * change
        hyw[s] = hyw[s] + (strip + strip_next)
        for x in range(-1, BX + 1):
            value = w[t, x + 2, s]
            edge = unpack_row(north, 0) if x < 0 else unpack_row(south, BX - 1) if x == BX else unpack_row(strip, x)
            west = jnp.where(first_lane, edge, pltpu.roll(value, 1, 1))
            east = jnp.where(last_lane, edge, pltpu.roll(value, LANES - 1, 1))
            change = (
                (coef[x + 1, 0] * w[t, x + 1, s] + coef[x + 1, 1] * w[t, x + 3, s])
                + (coef[x + 1, 2] * west + coef[x + 1, 3] * east)
                - coef[x + 1, 4] * value
            )
            if 0 <= x < BX:
                moved = adj[x, s] + change
                adj[x, s] = moved
                after = moved * ia[x + 1, s]
                wacc[x + 1, s] = wacc[x + 1, s] + after
            else:
                after = value + ia[x + 1, s] * change
                wacc[x + 1, s] = wacc[x + 1, s] + (value + after)
            w[t + 1, x + 2, s] = after
        return strip_next

    @pl.loop(0, SPEC)
    def _(s):
        for copy in exchange(0, 0, s, False):
            copy.wait_recv()
        halo = align(hyl[0, s, 0], hyr[0, s, 0])
        hyw[s] = halo
        wacc[0, s] = w[0, 1, s]
        wacc[BX + 1, s] = w[0, BX + 2, s]
        narrow(0, s, halo, 1)

    ts_rows = range(BX)
    for i in range(6):
        ts[i] = pack([tau[x + 1, i] for x in ts_rows])
    for copy in third:
        copy.start()
    for copy in second:
        copy.wait_recv()

    @pl.loop(0, (ROUNDS - 2) * SPEC)
    def _(i):
        e = i // SPEC + 1
        s = i % SPEC
        t = 2 * e - 1
        narrow(t + 1, s, wide(t, s, e), e + 1)

    @pl.loop(0, SPEC)
    def _(s):
        e = ROUNDS - 1
        t = SUB - 1
        for copy in exchange(e, t, s, True):
            copy.wait_recv()
        halo = align(hyl[e, s, 0], hyr[e, s, 0])
        hyw[s] = hyw[s] + halo
        wacc[0, s] = wacc[0, s] + w[t, 1, s]
        wacc[BX + 1, s] = wacc[BX + 1, s] + w[t, BX + 2, s]
        narrow(t, s, halo, None)

    writes = []
    for x in range(BX):
        copy = pltpu.make_async_copy(adj.at[x], out_h.at[:, :, x, :], in_sems.at[0, x])
        copy.start()
        writes.append(copy)

    for copy in setup[6:]:
        copy.wait_recv()
    flag_edge = pack([jnp.where(first_lane, up[x, 2], up[x, 3]).astype(F32) for x in range(BX)])
    flag_edge = pltpu.roll(flag_edge, LANES - 1, 1) == 1.0
    face_edge = zero_tile
    for s in range(SPEC):
        sum_halo = hyw[s]
        sum_own = pltpu.roll(pack([wacc[x + 1, s] for x in range(BX)]), LANES - 1, 1)
        conc_halo = align(psl[2 + s], psr[2 + s])
        conc_own = pltpu.roll(ps[2 + s], LANES - 1, 1)
        low = jnp.where(even, conc_halo, conc_own)
        high = jnp.where(even, conc_own, conc_halo)
        rise = jnp.where(even, sum_own - sum_halo, sum_halo - sum_own)
        face_edge = face_edge + jnp.where(flag_edge, low, high) * rise

    def x_face(x):
        flag = (up[x, 0] if x < BX else up[x - 1, 1]) == 1
        total = None
        for s in range(SPEC):
            term = jnp.where(flag, conc[x, s], conc[x + 1, s]) * (wacc[x + 1, s] - wacc[x, s])
            total = term if total is None else total + term
        return total

    before = x_face(0)
    fresh = []
    for x in range(BX):
        after = x_face(x + 1)
        flag = up[x, 3] == 1
        east = None
        for s in range(SPEC):
            here = conc[x + 1, s]
            mine = wacc[x + 1, s]
            term = jnp.where(flag, here, pltpu.roll(here, LANES - 1, 1)) * (pltpu.roll(mine, LANES - 1, 1) - mine)
            east = term if east is None else east + term
        edge = unpack_row(face_edge, x)
        west = jnp.where(first_lane, edge, pltpu.roll(east, 1, 1))
        east = jnp.where(last_lane, edge, east)
        faces = (before, after, west, east)
        start = None
        slope = None
        for i in range(4):
            one = st[i, x] * faces[i]
            two = jnp.abs(kk[i, x]) * faces[i]
            start = one if start is None else start + one
            slope = two if slope is None else slope + two
        grad[x] = STEP * slope
        d[0, x + 2] = start
        r[x] = start
        fresh.append(start)
        before = after
    dpy[0, 0] = pack(fresh)
    dpy[0, 1] = pack_second(fresh)
    for copy in cheb_exchange(0):
        copy.start()

    for copy in third:
        copy.wait_recv()
    ratios = [align(tl[i], tr[i]) for i in range(6)]

    def row_sides(field, x, edge):
        value = field(x)
        return (
            field(x - 1),
            field(x + 1),
            jnp.where(first_lane, edge, pltpu.roll(value, 1, 1)),
            jnp.where(last_lane, edge, pltpu.roll(value, LANES - 1, 1)),
            pltpu.roll(value, 1, 0),
            pltpu.roll(value, NZ - 1, 0),
        )

    def sweep(j, x, edge, residue, mix):
        value = d[j, x + 2]
        residue = residue - value
        for i, near in enumerate(row_sides(lambda y: d[j, y + 2], x, edge)):
            residue = residue + tau[x + 1, i] * near
        return residue, mix[0] * value + mix[1] * residue

    mixes = []
    rho = CONTRACT
    for j in range(CHEB - 1):
        rho_next = 1.0 / (2.0 / CONTRACT - rho)
        mixes.append((rho_next * rho, 2.0 * rho_next / CONTRACT))
        rho = rho_next
    back = 1.0 / mixes[1][1]

    def wide_sweep(j, strip_before):
        e = j // 2
        mix = mixes[j]
        for copy in cheb_exchange(e):
            copy.wait_recv()
        strip = align(dhl[e, 0], dhr[e, 0])
        further = align_second(dhl[e, 1], dhr[e, 1])
        north, south = corners(dhc[e, 0], dhc[e, 1], dhc[e, 2], dhc[e, 3])
        sides = strip_sides(strip, further, pltpu.roll(dpy[e, 0], LANES - 1, 1), north, south)
        floor = iota((8, LANES), 0)
        lower = pltpu.roll(strip, 1, 0)
        lower = jnp.where(floor == 0, pltpu.roll(lower, 2, 1), lower)
        upper = pltpu.roll(strip, 7, 0)
        upper = jnp.where(floor == 7, pltpu.roll(upper, LANES - 2, 1), upper)
        residue = strip if j == 0 else back * (strip - mixes[1][0] * strip_before)
        residue = residue - strip
        for i, near in enumerate(sides + (lower, upper)):
            residue = residue + ratios[i] * near
        strip_next = mix[0] * strip + mix[1] * residue
        for x in range(-1, BX + 1):
            edge = unpack_row(north, 0) if x < 0 else unpack_row(south, BX - 1) if x == BX else unpack_row(strip, x)
            if 0 <= x < BX:
                start = r[x]
            elif j == 0:
                start = d[j, x + 2]
            else:
                start = back * (d[j, x + 2] - mixes[1][0] * d[1, x + 2])
            residue, value = sweep(j, x, edge, start, mix)
            if 0 <= x < BX and j == 0:
                r[x] = residue
            d[j + 1, x + 2] = value
        return strip, strip_next

    strips = wide_sweep(0, None)
    fresh = []
    for x in range(BX):
        residue, value = sweep(1, x, unpack_row(strips[1], x), r[x], mixes[1])
        r[x] = residue
        d[2, x + 2] = value
        fresh.append(value)
    dpy[1, 0] = pack(fresh)
    dpy[1, 1] = pack_second(fresh)
    for copy in cheb_exchange(1):
        copy.start()
    strips += wide_sweep(2, strips[1])

    halo = (strips[0] + strips[1]) + (strips[2] + strips[3])
    for x in range(-1, BX + 1):
        m[x + 1] = (d[0, x + 2] + d[1, x + 2]) + (d[2, x + 2] + d[3, x + 2])
    for x in range(BX):
        value = m[x + 1]
        total = grad[x]
        for i, near in enumerate(row_sides(lambda y: m[y + 1], x, unpack_row(halo, x))):
            total = total - kk[i, x] * (value - near)
        grad[x] = total
        copy = pltpu.make_async_copy(grad.at[x], grad_h.at[:, x, :], in_sems.at[1, x])
        copy.start()
        writes.append(copy)

    for copy in setup + second + third:
        copy.wait_send()
    for e in range(2):
        for copy in cheb_exchange(e):
            copy.wait_send()

    @pl.loop(0, SPEC)
    def _(s):
        for copy in exchange(0, 0, s, False):
            copy.wait_send()

    @pl.loop(SPEC, ROUNDS * SPEC)
    def _(i):
        e = i // SPEC
        for copy in exchange(e, 2 * e - 1, i % SPEC, True):
            copy.wait_send()

    for copy in writes:
        copy.wait()


def body(adjoint_in, conc, pressure, perm, porosity, storage, rock, upwind, sorption):
    def vmem(*shape, dtype=F32):
        return pltpu.VMEM(shape, dtype)

    row = (NZ, LANES)
    tile = (8, LANES)
    hbm = pl.BlockSpec(memory_space=pltpu.HBM)
    return tuple(pl.pallas_call(
        kernel,
        out_shape=(
            jax.ShapeDtypeStruct(adjoint_in.shape, F32),
            jax.ShapeDtypeStruct(pressure.shape, F32),
        ),
        in_specs=[hbm] * 8 + [hbm],
        out_specs=(hbm, hbm),
        scratch_shapes=[
            vmem(BX, SPEC, *row),
            vmem(BX + 2, SPEC, *row),
            vmem(BX + 2, *row),
            vmem(BX + 2, *row),
            vmem(BX, *row),
            vmem(BX, *row),
            vmem(BX, *row, dtype=jnp.int32),
            vmem(BX, 4, *row, dtype=jnp.int32),
            vmem(BX + 2, SPEC, *row),
            vmem(SUB, BX + 4, SPEC, *row),
            vmem(BX + 2, SPEC, *row),
            vmem(ROUNDS, SPEC, 2, *tile),
            vmem(ROUNDS, SPEC, 2, *tile),
            vmem(ROUNDS, SPEC, 2, *tile),
            vmem(SPEC, *tile),
            vmem(ROUNDS, SPEC, 4, *tile),
            vmem(2 + SPEC, *tile),
            vmem(2 + SPEC, *tile),
            vmem(2 + SPEC, *tile),
            vmem(4 + SPEC, *tile),
            vmem(4 + SPEC, *tile),
            vmem(4 + SPEC, *tile),
            vmem(6, *tile),
            vmem(6, *tile),
            vmem(6, *tile),
            vmem(BX + 2, 5, *row),
            vmem(BX + 2, 6, *row),
            vmem(4, BX, *row),
            vmem(6, BX, *row),
            vmem(CHEB, BX + 4, *row),
            vmem(2, 2, *tile),
            vmem(2, 2, *tile),
            vmem(2, 2, *tile),
            vmem(2, 4, *tile),
            vmem(BX + 2, *row),
            vmem(BX, *row),
            vmem(BX, *row),
            pltpu.SMEM((2, SPEC, ROCKS), F32),
            pltpu.SemaphoreType.DMA((9, BX)),
            pltpu.SemaphoreType.DMA((SLOTS, 8)),
            pltpu.SemaphoreType.DMA((SLOTS, 8)),
        ],
        compiler_params=pltpu.CompilerParams(
            collective_id=0, has_side_effects=True, vmem_limit_bytes=63 * 2**20),
    )(adjoint_in, conc, pressure, perm, porosity, storage, rock, upwind, jnp.transpose(sorption, (0, 2, 1))))


def solution(mesh):
    in_specs = (
        P(None, None, "gx", "gy"),
        P(None, None, "gx", "gy"),
        P(None, "gx", "gy"),
        P(None, "gx", "gy"),
        P(None, "gx", "gy"),
        P(None, "gx", "gy"),
        P(None, "gx", "gy"),
        P(None, None, "gx", "gy"),
        P(),
    )
    out_specs = (P(None, None, "gx", "gy"), P(None, "gx", "gy"))
    return jax.shard_map(body, mesh=mesh, in_specs=in_specs, out_specs=out_specs, check_vma=False)
```

time: 88.8 us -> 69.9 us (0.79)
  Pallas kernels: 77.4 us -> 66.3 us
  local copies, waits for them, and re-layouts: 10.4 us -> 2.78 us
    pallas_call x1, Pallas kernels: 77.4 us -> 66.3 us  [body(): pl.pallas_call(kernel, out_shape=(jax.ShapeDtypeStruct(adjoint_in.shape,...]
    unnamed x19 -> x4, local copies, waits for them, and re-layouts: 10.4 us -> 2.78 us
where the time goes in v1:
time: 69.9 us; the launch traced here: 69.8 us
  Pallas kernels  66.3 us (95%)
  local copies, waits for them, and re-layouts  2.78 us (4%)
    pallas_call x1, Pallas kernels, body(): pl.pallas_call(kernel, out_shape=(jax.ShapeDtypeStruct(adjoint_in.shape,...  66.3 us
    unnamed x4, local copies, waits for them, and re-layouts  2.78 us

profile of v1, /device:TPU:1, one launch (start us, length us, event | category | flops | bytes accessed | tf_op | source)
XLA Modules:
  0.0 69.8 jit_solution(13026160029521278941)
XLA Ops:
  0.6 66.3 %shard_map.104 = (f32[4,48,8,128]{3,2,1,0:T(8,128)}, f32[48,8,128]{2,1,0:T(8,128)}) custom-call(f32[4,48,8,128]{3,2,1,0:T(8,128)} %adj_h.1, f32[4,48,8,128]{3,2,1,0:T(8,128)} %conc_h.1, f32[48,8,128]{2,1,0:T(8,128)} %press_h.1, f32[48,8,128]{2,1,0:T(8,128)} %perm_h.1, f32[48,8,128]{2,1,0:T(8,128)} %por_h.1, f32[48,8,128]{2,1,0:T(8,128)} %sto_h.1, ...), custom_call_target="tpu_custom_call" | custom-call | tf_op jit(solution)/shard_map/pallas_call | solution.py:592
  67.0 0.0 copy-start
  67.0 2.1 %copy.13 = f32[4,48,8,128]{3,2,1,0:T(8,128)} copy(f32[4,48,8,128]{3,2,1,0:T(8,128)} %get-tuple-element.4) | data formatting | bytes 1572864
  69.1 0.0 copy-done
  69.1 0.7 copy.14
Async XLA Ops:
  67.0 2.1 %copy-start = (f32[48,8,128]{2,1,0:T(8,128)S(1)}, f32[48,8,128]{2,1,0:T(8,128)}, u32[]{:S(2)}) copy-start(f32[48,8,128]{2,1,0:T(8,128)} %get-tuple-element.5) | copy-start | bytes 589828

commit v2 on v1

v2 whole, which is shorter than its diff:
```python
import jax
import jax.numpy as jnp
from jax import lax
from jax.experimental import pallas as pl
from jax.experimental.pallas import tpu as pltpu
from jax.sharding import PartitionSpec as P

ROCKS = 8
SUB = 8
CHEB = 4
SPEC = 4
NZ = 48
BX = 8
LANES = 128
ZT = NZ // 8
STEP = 0.02
CONTRACT = 0.9
F32 = jnp.float32
MESH = pl.DeviceIdType.MESH

ROUNDS = SUB // 2

CHEB_SLOT = ROUNDS * SPEC
PERM_SLOT = CHEB_SLOT + 2
PRESS_SLOT = PERM_SLOT + 1
CONC_SLOT = PERM_SLOT + 2
FLAG_SLOT = PERM_SLOT + 3
TAU_SLOT = PERM_SLOT + 4
AREA_SLOT = PERM_SLOT + 5
SLOTS = AREA_SLOT + SPEC


def iota(shape, dim):
    return lax.broadcasted_iota(jnp.int32, shape, dim)


HALF = BX // 2
ROW_LANES = 4 * ZT


def pack_tile(values, t, packed):
    u = t % (HALF * ZT)
    if u == 0:
        return values
    index = (iota((8, LANES), 1) + 2) % LANES // 4
    return jnp.where(index >= u, pltpu.roll(values, 4 * u, 1), packed)


def pack_row(values, x, packed):
    part = packed[x // HALF]
    for zt in range(ZT):
        part = pack_tile(values[8 * zt:8 * zt + 8], x * ZT + zt, part)
    return (part, packed[1]) if x < HALF else (packed[0], part)


def unpack_row(packed, x):
    part = packed[x // HALF]
    tiles = []
    for zt in range(ZT):
        u = (x % HALF) * ZT + zt
        tiles.append(pltpu.roll(part, LANES - 4 * u, 1) if u else part)
    return jnp.concatenate(tiles, axis=0)


def from_left():
    return iota((8, LANES), 1) % 4 == 0


def align(left, right):
    return tuple(
        jnp.where(from_left(), pltpu.roll(left[h], 1, 1), pltpu.roll(right[h], LANES - 1, 1)) for h in range(2))


def align_second(left, right):
    return tuple(
        jnp.where(from_left(), pltpu.roll(left[h], 2, 1), pltpu.roll(right[h], LANES - 2, 1)) for h in range(2))


def corners(tiles):
    shift = ROW_LANES * (HALF - 1)
    north = jnp.where(
        from_left(), pltpu.roll(tiles[0], LANES - shift + 1, 1), pltpu.roll(tiles[1], LANES - shift - 1, 1))
    south = jnp.where(from_left(), pltpu.roll(tiles[2], shift + 1, 1), pltpu.roll(tiles[3], shift - 1, 1))
    return (north, None), (None, south)


def strip_sides(strip, second, own, north, south):
    lane = iota((8, LANES), 1)
    shift = ROW_LANES * (HALF - 1)
    top = (lane + 1) % LANES < ROW_LANES
    bottom = (lane >= shift - 1) & (lane < shift - 1 + ROW_LANES)
    above = (
        jnp.where(top, north[0], pltpu.roll(strip[0], ROW_LANES, 1)),
        jnp.where(top, pltpu.roll(strip[0], LANES - shift, 1), pltpu.roll(strip[1], ROW_LANES, 1)),
    )
    below = (
        jnp.where(bottom, pltpu.roll(strip[1], shift, 1), pltpu.roll(strip[0], LANES - ROW_LANES, 1)),
        jnp.where(bottom, south[1], pltpu.roll(strip[1], LANES - ROW_LANES, 1)),
    )
    west = tuple(jnp.where(from_left(), second[h], own[h]) for h in range(2))
    east = tuple(jnp.where(from_left(), own[h], second[h]) for h in range(2))
    return above, below, west, east


def kernel(adj_h, conc_h, press_h, perm_h, por_h, sto_h, rock_h, up_h, sorp_h, out_h, grad_h,
           adj, conc, press, perm, por, sto, rock, up, ia, w, wacc, py, hyl, hyr, hyw,
           hc, ps, psl, psr, cs, cl, cr, vs, vl, vr, fs, fl, fr, qs, hp, ts, tl, tr,
           coef, trans, tau, st, kk, d, dpy, dhl, dhr, dhc,
           m, r, grad, sorp, in_sems, send, recv):
    gx = lax.axis_index("gx")
    gy = lax.axis_index("gy")
    nx = lax.axis_size("gx")
    ny = lax.axis_size("gy")
    to = [
        {"gx": lax.rem(gx + nx - 1, nx), "gy": gy},
        {"gx": lax.rem(gx + 1, nx), "gy": gy},
        {"gx": gx, "gy": lax.rem(gy + ny - 1, ny)},
        {"gx": gx, "gy": lax.rem(gy + 1, ny)},
    ]
    to += [{"gx": a["gx"], "gy": b["gy"]} for a in to[:2] for b in to[2:]]

    loads = {}

    def load(i, name, src, dst):
        loads[name] = []
        for x in range(BX):
            copy = pltpu.make_async_copy(src(x), dst(x), in_sems.at[i, x])
            copy.start()
            loads[name].append(copy)

    def arrived(*names):
        for name in names:
            for copy in loads[name]:
                copy.wait()

    barrier = pltpu.get_barrier_semaphore()
    for target in to:
        pl.semaphore_signal(barrier, inc=1, device_id=target, device_id_type=MESH)
    table = pltpu.make_async_copy(sorp_h, sorp, in_sems.at[8, 0])
    table.start()
    load(0, "conc", lambda x: conc_h.at[:, :, x, :], lambda x: conc.at[x + 1])
    load(1, "rock", lambda x: rock_h.at[:, x, :], lambda x: rock.at[x])
    load(2, "por", lambda x: por_h.at[:, x, :], lambda x: por.at[x])
    load(3, "adj", lambda x: adj_h.at[:, :, x, :], lambda x: adj.at[x])
    load(4, "perm", lambda x: perm_h.at[:, x, :], lambda x: perm.at[x + 2])
    load(5, "press", lambda x: press_h.at[:, x, :], lambda x: press.at[x + 2])
    load(6, "up", lambda x: up_h.at[:, :, x, :], lambda x: up.at[x + 1])
    load(7, "sto", lambda x: sto_h.at[:, x, :], lambda x: sto.at[x])

    def message(slot, way, src, dst):
        return pltpu.make_async_remote_copy(
            src_ref=src, dst_ref=dst, send_sem=send.at[slot, way], recv_sem=recv.at[slot, way],
            device_id=to[way], device_id_type=MESH)

    def row_messages(slot, field):
        return [
            message(slot, 0, field(2), field(BX + 2)),
            message(slot, 1, field(BX), field(0)),
        ]

    def corner_messages(slot, own, there):
        return [message(slot, 4 + q, own(q // 2), there(3 - q)) for q in range(4)]

    def exchange(e, t, s):
        slot = e * SPEC + s
        copies = row_messages(slot, lambda x: w.at[t, pl.ds(x, 2), s])
        copies += columns(slot, py.at[e, s], hyl.at[e, s], hyr.at[e, s])
        return copies + corner_messages(slot, lambda h: py.at[e, s, h], lambda q: hc.at[e, s, q])

    def cheb_exchange(e):
        slot = CHEB_SLOT + e
        copies = row_messages(slot, lambda x: d.at[2 * e, pl.ds(x, 2)])
        copies += columns(slot, dpy.at[e], dhl.at[e], dhr.at[e])
        return copies + corner_messages(slot, lambda h: dpy.at[e, h], lambda q: dhc.at[e, q])

    def beside(slot, field):
        return [
            message(slot, 0, field.at[1], field.at[BX + 1]),
            message(slot, 1, field.at[BX], field.at[0]),
        ]

    def columns(slot, own, left, right):
        return [message(slot, 2, own, right), message(slot, 3, own, left)]

    press_rows = row_messages(PRESS_SLOT, lambda x: press.at[pl.ds(x, 2)])
    press_rows += corner_messages(PRESS_SLOT, lambda h: ps.at[1, h], lambda q: hp.at[1, q])
    perm_rows = row_messages(PERM_SLOT, lambda x: perm.at[pl.ds(x, 2)])
    perm_rows += corner_messages(PERM_SLOT, lambda h: ps.at[0, h], lambda q: hp.at[0, q])
    head_columns = columns(PERM_SLOT, ps, psl, psr)
    flag_rows = beside(FLAG_SLOT, up)
    flag_columns = columns(FLAG_SLOT, fs, fl, fr)
    conc_rows = beside(CONC_SLOT, conc)
    conc_columns = columns(CONC_SLOT, cs, cl, cr)
    area_rows = [
        [
            message(AREA_SLOT + s, 0, ia.at[1, s], ia.at[BX + 1, s]),
            message(AREA_SLOT + s, 1, ia.at[BX, s], ia.at[0, s]),
        ]
        for s in range(SPEC)
    ]
    area_columns = columns(AREA_SLOT, vs, vl, vr)
    tau_rows = beside(TAU_SLOT, tau)
    tau_columns = columns(TAU_SLOT, ts, tl, tr)

    def start(*groups):
        for group in groups:
            for copy in group:
                copy.start()

    def received(*groups):
        for group in groups:
            for copy in group:
                copy.wait_recv()

    def pack(rows):
        packed = (None, None)
        for x in range(BX):
            packed = pack_row(rows(x), x, packed)
        return packed

    def put(ref, *index, packed):
        for h in range(2):
            ref[(*index, h)] = packed[h]

    def get(ref, *index):
        return ref[(*index, 0)], ref[(*index, 1)]

    lane = iota((NZ, LANES), 1)
    first_lane = lane == 0
    last_lane = lane == LANES - 1
    level = iota((NZ, LANES), 0)

    table.wait()
    arrived("conc", "rock", "por", "adj")
    packs = [(None, None)] * SPEC
    area_packs = [(None, None)] * SPEC
    for x in range(BX):
        kind = rock[x]
        bits = [(kind // (1 << b)) % 2 == 1 for b in range(3)]

        def look_up(row, s):
            level_values = [sorp[row, s, i] for i in range(ROCKS)]
            for b in range(3):
                level_values = [
                    jnp.where(bits[b], level_values[2 * i + 1], level_values[2 * i])
                    for i in range(len(level_values) // 2)
                ]
            return level_values[0]

        hole = por[x]
        for s in range(SPEC):
            lang = look_up(0, s)
            cap = look_up(1, s)
            base = 1.0 + lang * conc[x + 1, s]
            base = base * base
            inv = base / (hole * (base + cap * lang))
            ia[x + 1, s] = inv
            first = adj[x, s] * inv
            w[0, x + 2, s] = first
            packs[s] = pack_row(first, x, packs[s])
            area_packs[s] = pack_row(inv, x, area_packs[s])
    for s in range(SPEC):
        put(py, 0, s, packed=packs[s])
        put(vs, s, packed=area_packs[s])
    nothing = jnp.zeros((NZ, LANES), F32)
    for x in range(BX + 2):
        for s in range(SPEC):
            wacc[x, s] = nothing
    for s in range(SPEC):
        put(hyw, s, packed=(nothing[:8], nothing[:8]))
    arrived("perm", "press", "up")
    put(ps, 0, packed=pack(lambda x: perm[x + 2]))
    put(ps, 1, packed=pack(lambda x: press[x + 2]))
    for i in range(4):
        put(fs, i, packed=pack(lambda x: up[x + 1, i].astype(F32)))

    pl.semaphore_wait(barrier, 8)
    start(perm_rows, press_rows, head_columns, flag_columns, flag_rows, area_columns)
    for s in range(SPEC):
        start(exchange(0, 0, s), area_rows[s])
    start(conc_rows)
    for s in range(SPEC):
        put(cs, s, packed=pack(lambda x: conc[x + 1, s]))
    start(conc_columns)

    received(perm_rows, press_rows, head_columns, flag_rows, flag_columns)

    def inside(pair, outside):
        return tuple(
            None if item is None else jnp.where(
                from_left(),
                jnp.where((gy == 0) | outside, 0.0, item),
                jnp.where((gy == ny - 1) | outside, 0.0, item),
            ) for item in pair)

    top_edge = gx == 0
    bottom_edge = gx == nx - 1
    perm_beside = align(get(psl, 0), get(psr, 0))
    press_beside = align(get(psl, 1), get(psr, 1))
    perm_edge = inside(perm_beside, False)
    perm_north, perm_south = corners([hp[0, q] for q in range(4)])
    perm_north = inside(perm_north, top_edge)
    perm_south = inside(perm_south, bottom_edge)
    press_north, press_south = corners([hp[1, q] for q in range(4)])

    def face(own, near, drop, flag, i):
        share = near / (own + near)
        item = 2.0 * own * share
        up_here = (flag == 1) if i in (1, 3) else (flag != 1)
        return share, item, jnp.where(up_here, STEP * item * jnp.abs(drop), 0.0)

    for x in range(-1, BX + 1):
        own = perm[x + 2]
        head = press[x + 2]
        perm_n = jnp.where(top_edge, 0.0, perm[x + 1]) if x == 0 else perm[x + 1]
        perm_s = jnp.where(bottom_edge, 0.0, perm[x + 3]) if x == BX - 1 else perm[x + 3]
        if x < 0:
            edge, head_edge = unpack_row(perm_north, 0), unpack_row(press_north, 0)
        elif x == BX:
            edge, head_edge = unpack_row(perm_south, BX - 1), unpack_row(press_south, BX - 1)
        else:
            edge, head_edge = unpack_row(perm_edge, x), unpack_row(press_beside, x)
        perm_w = jnp.where(first_lane, edge, pltpu.roll(own, 1, 1))
        perm_e = jnp.where(last_lane, edge, pltpu.roll(own, LANES - 1, 1))
        drops = (
            head - press[x + 1],
            head - press[x + 3],
            head - jnp.where(first_lane, head_edge, pltpu.roll(head, 1, 1)),
            head - jnp.where(last_lane, head_edge, pltpu.roll(head, LANES - 1, 1)),
        )
        centre = None
        for i, near in enumerate((perm_n, perm_s, perm_w, perm_e)):
            drop = drops[i]
            share, item, push = face(own, near, drop, up[x + 1, i], i)
            if 0 <= x < BX:
                trans[i, x] = item
                kk[i, x] = 2.0 * share * share * drop
                st[i, x] = STEP * jnp.where(drop > 0, item, jnp.where(drop < 0, -item, 0.0))
            coef[x + 1, i] = push
            centre = push if centre is None else centre + push
        coef[x + 1, 4] = centre

    perm_sides = strip_sides(
        perm_beside, align_second(get(psl, 0), get(psr, 0)), get(ps, 0), perm_north, perm_south)
    press_sides = strip_sides(
        press_beside, align_second(get(psl, 1), get(psr, 1)), get(ps, 1), press_north, press_south)
    for i in range(4):
        flag = align(get(fl, i), get(fr, i))
        put(qs, i, packed=tuple(
            face(perm_beside[h], perm_sides[i][h], press_beside[h] - press_sides[i][h], flag[h], i)[2]
            for h in range(2)))

    def repeat(t, s, first, last, edge, keep, store):
        above = w[t, first + 1, s]
        value = w[t, first + 2, s]
        for x in range(first, last):
            below = w[t, x + 3, s]
            beside_row = edge(x)
            west = jnp.where(first_lane, beside_row, pltpu.roll(value, 1, 1))
            east = jnp.where(last_lane, beside_row, pltpu.roll(value, LANES - 1, 1))
            change = (
                (coef[x + 1, 0] * above + coef[x + 1, 1] * below)
                + (coef[x + 1, 2] * west + coef[x + 1, 3] * east)
                - coef[x + 1, 4] * value
            )
            after = value + ia[x + 1, s] * change
            if store:
                w[t + 1, x + 2, s] = after
            keep(x, value, after)
            above, value = value, below

    def narrow(t, s, halo, e):
        packed = [(None, None)]

        def keep(x, value, after):
            packed[0] = pack_row(after, x, packed[0])

        repeat(t, s, 0, BX, lambda x: unpack_row(halo, x), keep, True)
        put(py, e, s, packed=packed[0])
        start(exchange(e, t + 1, s))

    def wide(t, s, e, store):
        received(exchange(e, t, s))
        strip = align(get(hyl, e, s), get(hyr, e, s))
        further = align_second(get(hyl, e, s), get(hyr, e, s))
        north, south = corners([hc[e, s, q] for q in range(4)])
        sides = strip_sides(strip, further, get(py, e, s), north, south)
        shares = [get(qs, i) for i in range(4)]
        scale = align(get(vl, s), get(vr, s))
        beyond = []
        for h in range(2):
            change = None
            for i in range(4):
                term = shares[i][h] * (sides[i][h] - strip[h])
                change = term if change is None else change + term
            after = strip[h] + scale[h] * change
            hyw[s, h] = hyw[s, h] + (strip[h] + after)
            beyond.append(after)

        def edge(x):
            return unpack_row(north, 0) if x < 0 else unpack_row(south, BX - 1) if x == BX else unpack_row(strip, x)

        def keep(x, value, after):
            wacc[x + 1, s] = wacc[x + 1, s] + (value + after)

        repeat(t, s, -1, BX + 1, edge, keep, store)
        return beyond

    received(area_columns)
    for s in range(SPEC):
        received(area_rows[s])
        narrow(1, s, wide(0, s, 0, True), 1)

    arrived("sto")
    packs = [(None, None)] * 6
    for x in range(BX):
        own = perm[x + 2]
        head = press[x + 2]
        items = [trans[i, x] for i in range(4)]
        for i, turn, end in ((4, 1, 0), (5, NZ - 1, NZ - 1)):
            near = jnp.where(level == end, 0.0, pltpu.roll(own, turn, 0))
            share = near / (own + near)
            items.append(2.0 * own * share)
            kk[i, x] = 2.0 * share * share * (head - pltpu.roll(head, turn, 0))
        total = sto[x]
        for item in items:
            total = total + item
        inv_diag = 1.0 / total
        for i in range(6):
            ratio = items[i] * inv_diag
            tau[x + 1, i] = ratio
            packs[i] = pack_row(ratio, x, packs[i])
            if i < 4:
                st[i, x] = st[i, x] * inv_diag
    for i in range(6):
        put(ts, i, packed=packs[i])
    start(tau_rows, tau_columns)

    @pl.loop(SPEC, (ROUNDS - 1) * SPEC)
    def _(i):
        e = i // SPEC
        s = i % SPEC
        narrow(2 * e + 1, s, wide(2 * e, s, e, True), e + 1)

    @pl.loop(0, SPEC)
    def _(s):
        wide(SUB - 2, s, ROUNDS - 1, False)

    received(conc_rows, conc_columns)
    writes = []

    conc_edge = [align(get(cl, s), get(cr, s)) for s in range(SPEC)]

    def x_face(x):
        flag = (up[x + 1, 0] if x < BX else up[x, 1]) == 1
        total = None
        for s in range(SPEC):
            term = jnp.where(flag, conc[x, s], conc[x + 1, s]) * (wacc[x + 1, s] - wacc[x, s])
            total = term if total is None else total + term
        return total

    before = x_face(0)
    packed = (None, None)
    for x in range(BX):
        after = x_face(x + 1)
        flag_west = up[x + 1, 2] == 1
        flag_east = up[x + 1, 3] == 1
        east = None
        for s in range(SPEC):
            here = conc[x + 1, s]
            mine = wacc[x + 1, s]
            here_edge = unpack_row(conc_edge[s], x)
            mine_edge = unpack_row(get(hyw, s), x)
            near = jnp.where(last_lane, here_edge, pltpu.roll(here, LANES - 1, 1))
            rise = jnp.where(last_lane, mine_edge, pltpu.roll(mine, LANES - 1, 1)) - mine
            term = jnp.where(flag_east, here, near) * rise
            east = term if east is None else east + term
            term = jnp.where(flag_west, here_edge, here) * (mine - mine_edge)
            west = term if s == 0 else west + term
        west = jnp.where(first_lane, west, pltpu.roll(east, 1, 1))
        faces = (before, after, west, east)
        start_row = None
        slope = None
        for i in range(4):
            one = st[i, x] * faces[i]
            two = jnp.abs(kk[i, x]) * faces[i]
            start_row = one if start_row is None else start_row + one
            slope = two if slope is None else slope + two
        grad[x] = STEP * slope
        d[0, x + 2] = start_row
        r[x] = start_row
        packed = pack_row(start_row, x, packed)
        before = after
    put(dpy, 0, packed=packed)
    start(cheb_exchange(0))

    for x in range(BX):
        for s in range(SPEC):
            value = wacc[x + 1, s]
            beside_row = unpack_row(get(hyw, s), x)
            west = jnp.where(first_lane, beside_row, pltpu.roll(value, 1, 1))
            east = jnp.where(last_lane, beside_row, pltpu.roll(value, LANES - 1, 1))
            adj[x, s] = adj[x, s] + (
                (coef[x + 1, 0] * wacc[x, s] + coef[x + 1, 1] * wacc[x + 2, s])
                + (coef[x + 1, 2] * west + coef[x + 1, 3] * east)
                - coef[x + 1, 4] * value
            )
        copy = pltpu.make_async_copy(adj.at[x], out_h.at[:, :, x, :], in_sems.at[0, x])
        copy.start()
        writes.append(copy)

    received(tau_rows, tau_columns)
    ratios = [align(get(tl, i), get(tr, i)) for i in range(6)]

    def row_sides(field, x, edge):
        value = field(x)
        return (
            field(x - 1),
            field(x + 1),
            jnp.where(first_lane, edge, pltpu.roll(value, 1, 1)),
            jnp.where(last_lane, edge, pltpu.roll(value, LANES - 1, 1)),
            pltpu.roll(value, 1, 0),
            pltpu.roll(value, NZ - 1, 0),
        )

    def sweep(j, x, edge, residue, mix):
        value = d[j, x + 2]
        residue = residue - value
        for i, near in enumerate(row_sides(lambda y: d[j, y + 2], x, edge)):
            residue = residue + tau[x + 1, i] * near
        return residue, mix[0] * value + mix[1] * residue

    mixes = []
    rho = CONTRACT
    for j in range(CHEB - 1):
        rho_next = 1.0 / (2.0 / CONTRACT - rho)
        mixes.append((rho_next * rho, 2.0 * rho_next / CONTRACT))
        rho = rho_next
    back = 1.0 / mixes[1][1]

    def wide_sweep(j, strip_before):
        e = j // 2
        mix = mixes[j]
        received(cheb_exchange(e))
        strip = align(get(dhl, e), get(dhr, e))
        further = align_second(get(dhl, e), get(dhr, e))
        north, south = corners([dhc[e, q] for q in range(4)])
        sides = strip_sides(strip, further, get(dpy, e), north, south)
        floor = iota((8, LANES), 0)
        beyond = []
        for h in range(2):
            lower = pltpu.roll(strip[h], 1, 0)
            lower = jnp.where(floor == 0, pltpu.roll(lower, 4, 1), lower)
            upper = pltpu.roll(strip[h], 7, 0)
            upper = jnp.where(floor == 7, pltpu.roll(upper, LANES - 4, 1), upper)
            residue = strip[h] if j == 0 else back * (strip[h] - mixes[1][0] * strip_before[h])
            residue = residue - strip[h]
            for i, near in enumerate([side[h] for side in sides] + [lower, upper]):
                residue = residue + ratios[i][h] * near
            beyond.append(mix[0] * strip[h] + mix[1] * residue)
        for x in range(-1, BX + 1):
            edge = unpack_row(north, 0) if x < 0 else unpack_row(south, BX - 1) if x == BX else unpack_row(strip, x)
            if 0 <= x < BX:
                begin = r[x]
            elif j == 0:
                begin = d[j, x + 2]
            else:
                begin = back * (d[j, x + 2] - mixes[1][0] * d[1, x + 2])
            residue, value = sweep(j, x, edge, begin, mix)
            if 0 <= x < BX and j == 0:
                r[x] = residue
            d[j + 1, x + 2] = value
        return strip, tuple(beyond)

    strips = wide_sweep(0, None)
    packed = (None, None)
    for x in range(BX):
        residue, value = sweep(1, x, unpack_row(strips[1], x), r[x], mixes[1])
        r[x] = residue
        d[2, x + 2] = value
        packed = pack_row(value, x, packed)
    put(dpy, 1, packed=packed)
    start(cheb_exchange(1))
    strips += wide_sweep(2, strips[1])

    halo = tuple((strips[0][h] + strips[1][h]) + (strips[2][h] + strips[3][h]) for h in range(2))
    for x in range(-1, BX + 1):
        m[x + 1] = (d[0, x + 2] + d[1, x + 2]) + (d[2, x + 2] + d[3, x + 2])
    for x in range(BX):
        value = m[x + 1]
        total = grad[x]
        for i, near in enumerate(row_sides(lambda y: m[y + 1], x, unpack_row(halo, x))):
            total = total - kk[i, x] * (value - near)
        grad[x] = total
        copy = pltpu.make_async_copy(grad.at[x], grad_h.at[:, x, :], in_sems.at[1, x])
        copy.start()
        writes.append(copy)

    for group in [perm_rows, press_rows, head_columns, conc_rows, conc_columns, area_columns,
                  flag_rows, flag_columns, tau_rows, tau_columns] + area_rows:
        for copy in group:
            copy.wait_send()
    for e in range(2):
        for copy in cheb_exchange(e):
            copy.wait_send()

    @pl.loop(0, ROUNDS * SPEC)
    def _(i):
        e = i // SPEC
        for copy in exchange(e, 2 * e, i % SPEC):
            copy.wait_send()

    for copy in writes:
        copy.wait()


def hand_over(adj, grad, adj_out, grad_out, adj_there, grad_there, sems):
    parts = [(adj.at[s], adj_there.at[s], adj_out.at[s]) for s in range(SPEC)] + [(grad, grad_there, grad_out)]
    inward = [pltpu.make_async_copy(a, b, sems.at[0, i]) for i, (a, b, c) in enumerate(parts)]
    outward = [pltpu.make_async_copy(b, c, sems.at[1, i]) for i, (a, b, c) in enumerate(parts)]
    for copy in inward:
        copy.start()
    for first, second in zip(inward, outward):
        first.wait()
        second.start()
    for copy in outward:
        copy.wait()


def body(adjoint_in, conc, pressure, perm, porosity, storage, rock, upwind, sorption):
    def vmem(*shape, dtype=F32):
        return pltpu.VMEM(shape, dtype)

    row = (NZ, LANES)
    tile = (8, LANES)
    hbm = pl.BlockSpec(memory_space=pltpu.HBM)
    adjoint_out, grad = pl.pallas_call(
        kernel,
        out_shape=(
            jax.ShapeDtypeStruct(adjoint_in.shape, F32),
            jax.ShapeDtypeStruct(pressure.shape, F32),
        ),
        in_specs=[hbm] * 8 + [hbm],
        out_specs=(hbm, hbm),
        scratch_shapes=[
            vmem(BX, SPEC, *row),
            vmem(BX + 2, SPEC, *row),
            vmem(BX + 4, *row),
            vmem(BX + 4, *row),
            vmem(BX, *row),
            vmem(BX, *row),
            vmem(BX, *row, dtype=jnp.int32),
            vmem(BX + 2, 4, *row, dtype=jnp.int32),
            vmem(BX + 2, SPEC, *row),
            vmem(SUB, BX + 4, SPEC, *row),
            vmem(BX + 2, SPEC, *row),
            vmem(ROUNDS, SPEC, 2, *tile),
            vmem(ROUNDS, SPEC, 2, *tile),
            vmem(ROUNDS, SPEC, 2, *tile),
            vmem(SPEC, 2, *tile),
            vmem(ROUNDS, SPEC, 4, *tile),
        ] + [vmem(2, 2, *tile)] * 3 + [
        ] + [vmem(SPEC, 2, *tile)] * 10 + [
            vmem(2, 4, *tile),
        ] + [vmem(6, 2, *tile)] * 3 + [
            vmem(BX + 2, 5, *row),
            vmem(4, BX, *row),
            vmem(BX + 2, 6, *row),
            vmem(4, BX, *row),
            vmem(6, BX, *row),
            vmem(CHEB, BX + 4, *row),
            vmem(2, 2, *tile),
            vmem(2, 2, *tile),
            vmem(2, 2, *tile),
            vmem(2, 4, *tile),
            vmem(BX + 2, *row),
            vmem(BX, *row),
            vmem(BX, *row),
            pltpu.SMEM((2, SPEC, ROCKS), F32),
            pltpu.SemaphoreType.DMA((9, BX)),
            pltpu.SemaphoreType.DMA((SLOTS, 8)),
            pltpu.SemaphoreType.DMA((SLOTS, 8)),
        ],
        compiler_params=pltpu.CompilerParams(
            collective_id=0, has_side_effects=True, vmem_limit_bytes=63 * 2**20),
    )(adjoint_in, conc, pressure, perm, porosity, storage, rock, upwind, jnp.transpose(sorption, (0, 2, 1)))
    return tuple(pl.pallas_call(
        hand_over,
        out_shape=(
            jax.ShapeDtypeStruct(adjoint_in.shape, F32),
            jax.ShapeDtypeStruct(pressure.shape, F32),
        ),
        in_specs=[hbm] * 2,
        out_specs=(hbm, hbm),
        scratch_shapes=[
            vmem(*adjoint_in.shape),
            vmem(*pressure.shape),
            pltpu.SemaphoreType.DMA((2, SPEC + 1)),
        ],
        compiler_params=pltpu.CompilerParams(vmem_limit_bytes=63 * 2**20),
    )(adjoint_out, grad))


def solution(mesh):
    in_specs = (
        P(None, None, "gx", "gy"),
        P(None, None, "gx", "gy"),
        P(None, "gx", "gy"),
        P(None, "gx", "gy"),
        P(None, "gx", "gy"),
        P(None, "gx", "gy"),
        P(None, "gx", "gy"),
        P(None, None, "gx", "gy"),
        P(),
    )
    out_specs = (P(None, None, "gx", "gy"), P(None, "gx", "gy"))
    return jax.shard_map(body, mesh=mesh, in_specs=in_specs, out_specs=out_specs, check_vma=False)
```

time: 69.9 us -> 67.2 us (0.961)
  local copies, waits for them, and re-layouts: 2.78 us -> 0 us
    unnamed x4 -> x0, local copies, waits for them, and re-layouts: 2.78 us -> none
    pallas_call x0 -> x1, Pallas kernels: none -> 2.05 us  [body(): pl.pallas_call(hand_over, out_shape=(jax.ShapeDtypeStruct(adjoint_in.shap...]
    pallas_call x1, Pallas kernels: 66.3 us -> 64.3 us  [body(): pl.pallas_call(kernel, out_shape=(jax.ShapeDtypeStruct(adjoint_in.shape,...]
where the time goes in v2:
time: 67.2 us; the launch traced here: 67 us
  Pallas kernels  66.4 us (99%)
    pallas_call x1, Pallas kernels, body(): pl.pallas_call(kernel, out_shape=(jax.ShapeDtypeStruct(adjoint_in.shape,...  64.3 us
    pallas_call x1, Pallas kernels, body(): pl.pallas_call(hand_over, out_shape=(jax.ShapeDtypeStruct(adjoint_in.shap...  2.05 us

profile of v2, /device:TPU:1, one launch (start us, length us, event | category | flops | bytes accessed | tf_op | source)
XLA Modules:
  0.0 67.0 jit_solution(9034434928745171685)
XLA Ops:
  0.6 64.3 %shard_map.104 = (f32[4,48,8,128]{3,2,1,0:T(8,128)}, f32[48,8,128]{2,1,0:T(8,128)}) custom-call(f32[4,48,8,128]{3,2,1,0:T(8,128)} %adj_h.1, f32[4,48,8,128]{3,2,1,0:T(8,128)} %conc_h.1, f32[48,8,128]{2,1,0:T(8,128)} %press_h.1, f32[48,8,128]{2,1,0:T(8,128)} %perm_h.1, f32[48,8,128]{2,1,0:T(8,128)} %por_h.1, f32[48,8,128]{2,1,0:T(8,128)} %sto_h.1, ...), custom_call_target="tpu_custom_call" | custom-call | tf_op jit(solution)/shard_map/pallas_call | solution.py:637
  65.0 2.0 %shard_map.105 = (f32[4,48,8,128]{3,2,1,0:T(8,128)}, f32[48,8,128]{2,1,0:T(8,128)}) custom-call(f32[4,48,8,128]{3,2,1,0:T(8,128)} %get-tuple-element.4.adj, f32[48,8,128]{2,1,0:T(8,128)} %get-tuple-element.5.grad), custom_call_target="tpu_custom_call" | custom-call | tf_op jit(solution)/shard_map/pallas_call | solution.py:687

commit v3 on v2

--- a/solution.py
+++ b/solution.py
@@ -278,12 +278,10 @@
     start(perm_rows, press_rows, head_columns, flag_columns, flag_rows, area_columns)
     for s in range(SPEC):
         start(exchange(0, 0, s), area_rows[s])
-    start(conc_rows)
     for s in range(SPEC):
         put(cs, s, packed=pack(lambda x: conc[x + 1, s]))
-    start(conc_columns)
-
-    received(perm_rows, press_rows, head_columns, flag_rows, flag_columns)
+
+    received(perm_rows[:2], press_rows[:2], head_columns)
 
     def inside(pair, outside):
         return tuple(
@@ -298,18 +296,19 @@
     perm_beside = align(get(psl, 0), get(psr, 0))
     press_beside = align(get(psl, 1), get(psr, 1))
     perm_edge = inside(perm_beside, False)
-    perm_north, perm_south = corners([hp[0, q] for q in range(4)])
-    perm_north = inside(perm_north, top_edge)
-    perm_south = inside(perm_south, bottom_edge)
-    press_north, press_south = corners([hp[1, q] for q in range(4)])
-
     def face(own, near, drop, flag, i):
         share = near / (own + near)
         item = 2.0 * own * share
         up_here = (flag == 1) if i in (1, 3) else (flag != 1)
         return share, item, jnp.where(up_here, STEP * item * jnp.abs(drop), 0.0)
 
-    for x in range(-1, BX + 1):
+    for x in (*range(BX), -1, BX):
+        if x < 0:
+            received(perm_rows[2:], press_rows[2:], flag_rows, flag_columns)
+            perm_north, perm_south = corners([hp[0, q] for q in range(4)])
+            perm_north = inside(perm_north, top_edge)
+            perm_south = inside(perm_south, bottom_edge)
+            press_north, press_south = corners([hp[1, q] for q in range(4)])
         own = perm[x + 2]
         head = press[x + 2]
         perm_n = jnp.where(top_edge, 0.0, perm[x + 1]) if x == 0 else perm[x + 1]
@@ -380,8 +379,15 @@
         start(exchange(e, t + 1, s))
 
     def wide(t, s, e, store):
-        received(exchange(e, t, s))
+        copies = exchange(e, t, s)
+        received(copies[:4])
         strip = align(get(hyl, e, s), get(hyr, e, s))
+
+        def keep(x, value, after):
+            wacc[x + 1, s] = wacc[x + 1, s] + (value + after)
+
+        repeat(t, s, 0, BX, lambda x: unpack_row(strip, x), keep, store)
+        received(copies[4:])
         further = align_second(get(hyl, e, s), get(hyr, e, s))
         north, south = corners([hc[e, s, q] for q in range(4)])
         sides = strip_sides(strip, further, get(py, e, s), north, south)
@@ -396,14 +402,8 @@
             after = strip[h] + scale[h] * change
             hyw[s, h] = hyw[s, h] + (strip[h] + after)
             beyond.append(after)
-
-        def edge(x):
-            return unpack_row(north, 0) if x < 0 else unpack_row(south, BX - 1) if x == BX else unpack_row(strip, x)
-
-        def keep(x, value, after):
-            wacc[x + 1, s] = wacc[x + 1, s] + (value + after)
-
-        repeat(t, s, -1, BX + 1, edge, keep, store)
+        repeat(t, s, -1, 0, lambda x: unpack_row(north, 0), keep, store)
+        repeat(t, s, BX, BX + 1, lambda x: unpack_row(south, BX - 1), keep, store)
         return beyond
 
     received(area_columns)
@@ -441,6 +441,10 @@
         e = i // SPEC
         s = i % SPEC
         narrow(2 * e + 1, s, wide(2 * e, s, e, True), e + 1)
+
+        @pl.when(i == 2 * SPEC - 1)
+        def _():
+            start(conc_rows, conc_columns)
 
     @pl.loop(0, SPEC)
     def _(s):
@@ -541,8 +545,15 @@
     def wide_sweep(j, strip_before):
         e = j // 2
         mix = mixes[j]
-        received(cheb_exchange(e))
+        copies = cheb_exchange(e)
+        received(copies[:4])
         strip = align(get(dhl, e), get(dhr, e))
+        for x in range(BX):
+            residue, value = sweep(j, x, unpack_row(strip, x), r[x], mix)
+            if j == 0:
+                r[x] = residue
+            d[j + 1, x + 2] = value
+        received(copies[4:])
         further = align_second(get(dhl, e), get(dhr, e))
         north, south = corners([dhc[e, q] for q in range(4)])
         sides = strip_sides(strip, further, get(dpy, e), north, south)
@@ -558,17 +569,11 @@
             for i, near in enumerate([side[h] for side in sides] + [lower, upper]):
                 residue = residue + ratios[i][h] * near
             beyond.append(mix[0] * strip[h] + mix[1] * residue)
-        for x in range(-1, BX + 1):
-            edge = unpack_row(north, 0) if x < 0 else unpack_row(south, BX - 1) if x == BX else unpack_row(strip, x)
-            if 0 <= x < BX:
-                begin = r[x]
-            elif j == 0:
-                begin = d[j, x + 2]
-            else:
-                begin = back * (d[j, x + 2] - mixes[1][0] * d[1, x + 2])
+        for x, edge in ((-1, unpack_row(north, 0)), (BX, unpack_row(south, BX - 1))):
+            begin = d[j, x + 2]
+            if j:
+                begin = back * (begin - mixes[1][0] * d[1, x + 2])
             residue, value = sweep(j, x, edge, begin, mix)
-            if 0 <= x < BX and j == 0:
-                r[x] = residue
             d[j + 1, x + 2] = value
         return strip, tuple(beyond)
 

time: 67.2 us -> 66 us (0.982)
  Pallas kernels: 66.4 us -> 65.2 us
    pallas_call x1, Pallas kernels: 64.3 us -> 63.2 us  [body(): pl.pallas_call(kernel, out_shape=(jax.ShapeDtypeStruct(adjoint_in.shape,...]
where the time goes in v3:
time: 66 us; the launch traced here: 65.8 us
  Pallas kernels  65.2 us (99%)
    pallas_call x1, Pallas kernels, body(): pl.pallas_call(kernel, out_shape=(jax.ShapeDtypeStruct(adjoint_in.shape,...  63.2 us
    pallas_call x1, Pallas kernels, body(): pl.pallas_call(hand_over, out_shape=(jax.ShapeDtypeStruct(adjoint_in.shap...  2.05 us

profile of v3, /device:TPU:1, one launch (start us, length us, event | category | flops | bytes accessed | tf_op | source)
XLA Modules:
  0.0 65.8 jit_solution(13147591241845054470)
XLA Ops:
  0.6 63.2 %shard_map.104 = (f32[4,48,8,128]{3,2,1,0:T(8,128)}, f32[48,8,128]{2,1,0:T(8,128)}) custom-call(f32[4,48,8,128]{3,2,1,0:T(8,128)} %adj_h.1, f32[4,48,8,128]{3,2,1,0:T(8,128)} %conc_h.1, f32[48,8,128]{2,1,0:T(8,128)} %press_h.1, f32[48,8,128]{2,1,0:T(8,128)} %perm_h.1, f32[48,8,128]{2,1,0:T(8,128)} %por_h.1, f32[48,8,128]{2,1,0:T(8,128)} %sto_h.1, ...), custom_call_target="tpu_custom_call" | custom-call | tf_op jit(solution)/shard_map/pallas_call | solution.py:642
  63.8 2.0 %shard_map.105 = (f32[4,48,8,128]{3,2,1,0:T(8,128)}, f32[48,8,128]{2,1,0:T(8,128)}) custom-call(f32[4,48,8,128]{3,2,1,0:T(8,128)} %get-tuple-element.4.adj, f32[48,8,128]{2,1,0:T(8,128)} %get-tuple-element.5.grad), custom_call_target="tpu_custom_call" | custom-call | tf_op jit(solution)/shard_map/pallas_call | solution.py:692

commit v4 on v3

--- a/solution.py
+++ b/solution.py
@@ -36,6 +36,7 @@
 
 HALF = BX // 2
 ROW_LANES = 4 * ZT
+FLAG = (0, 3, 1, 2)
 
 
 def pack_tile(values, t, packed):
@@ -144,7 +145,9 @@
     load(3, "adj", lambda x: adj_h.at[:, :, x, :], lambda x: adj.at[x])
     load(4, "perm", lambda x: perm_h.at[:, x, :], lambda x: perm.at[x + 2])
     load(5, "press", lambda x: press_h.at[:, x, :], lambda x: press.at[x + 2])
-    load(6, "up", lambda x: up_h.at[:, :, x, :], lambda x: up.at[x + 1])
+    load(6, "up", lambda x: up_h.at[pl.ds(2, 2), :, x, :], lambda x: up.at[x + 1, pl.ds(1, 2)])
+    load(9, "up north", lambda x: up_h.at[0, :, x, :], lambda x: up.at[x + 1, 0])
+    load(10, "up south", lambda x: up_h.at[1, :, x, :], lambda x: up.at[x + 1, 3])
     load(7, "sto", lambda x: sto_h.at[:, x, :], lambda x: sto.at[x])
 
     def message(slot, way, src, dst):
@@ -187,7 +190,10 @@
     perm_rows = row_messages(PERM_SLOT, lambda x: perm.at[pl.ds(x, 2)])
     perm_rows += corner_messages(PERM_SLOT, lambda h: ps.at[0, h], lambda q: hp.at[0, q])
     head_columns = columns(PERM_SLOT, ps, psl, psr)
-    flag_rows = beside(FLAG_SLOT, up)
+    flag_rows = [
+        message(FLAG_SLOT, 0, up.at[1, pl.ds(1, 3)], up.at[BX + 1, pl.ds(1, 3)]),
+        message(FLAG_SLOT, 1, up.at[BX, pl.ds(0, 3)], up.at[0, pl.ds(0, 3)]),
+    ]
     flag_columns = columns(FLAG_SLOT, fs, fl, fr)
     conc_rows = beside(CONC_SLOT, conc)
     conc_columns = columns(CONC_SLOT, cs, cl, cr)
@@ -268,11 +274,11 @@
             wacc[x, s] = nothing
     for s in range(SPEC):
         put(hyw, s, packed=(nothing[:8], nothing[:8]))
-    arrived("perm", "press", "up")
+    arrived("perm", "press", "up", "up north", "up south")
     put(ps, 0, packed=pack(lambda x: perm[x + 2]))
     put(ps, 1, packed=pack(lambda x: press[x + 2]))
     for i in range(4):
-        put(fs, i, packed=pack(lambda x: up[x + 1, i].astype(F32)))
+        put(fs, i, packed=pack(lambda x: up[x + 1, FLAG[i]].astype(F32)))
 
     pl.semaphore_wait(barrier, 8)
     start(perm_rows, press_rows, head_columns, flag_columns, flag_rows, area_columns)
@@ -330,7 +336,12 @@
         centre = None
         for i, near in enumerate((perm_n, perm_s, perm_w, perm_e)):
             drop = drops[i]
-            share, item, push = face(own, near, drop, up[x + 1, i], i)
+            flag = up[x + 1, FLAG[i]]
+            if x < 0 and i == 1:
+                flag = up[1, FLAG[0]]
+            if x == BX and i == 0:
+                flag = up[BX, FLAG[1]]
+            share, item, push = face(own, near, drop, flag, i)
             if 0 <= x < BX:
                 trans[i, x] = item
                 kk[i, x] = 2.0 * share * share * drop
@@ -456,7 +467,7 @@
     conc_edge = [align(get(cl, s), get(cr, s)) for s in range(SPEC)]
 
     def x_face(x):
-        flag = (up[x + 1, 0] if x < BX else up[x, 1]) == 1
+        flag = (up[x + 1, FLAG[0]] if x < BX else up[x, FLAG[1]]) == 1
         total = None
         for s in range(SPEC):
             term = jnp.where(flag, conc[x, s], conc[x + 1, s]) * (wacc[x + 1, s] - wacc[x, s])
@@ -467,8 +478,8 @@
     packed = (None, None)
     for x in range(BX):
         after = x_face(x + 1)
-        flag_west = up[x + 1, 2] == 1
-        flag_east = up[x + 1, 3] == 1
+        flag_west = up[x + 1, FLAG[2]] == 1
+        flag_east = up[x + 1, FLAG[3]] == 1
         east = None
         for s in range(SPEC):
             here = conc[x + 1, s]
@@ -682,7 +693,7 @@
             vmem(BX, *row),
             vmem(BX, *row),
             pltpu.SMEM((2, SPEC, ROCKS), F32),
-            pltpu.SemaphoreType.DMA((9, BX)),
+            pltpu.SemaphoreType.DMA((11, BX)),
             pltpu.SemaphoreType.DMA((SLOTS, 8)),
             pltpu.SemaphoreType.DMA((SLOTS, 8)),
         ],

time: 66 us -> 65.6 us (level)
  no operation moved by 1% of the time
where the time goes in v4:
time: 65.6 us; the launch traced here: 65.5 us
  Pallas kernels  64.8 us (99%)
    pallas_call x1, Pallas kernels, body(): pl.pallas_call(kernel, out_shape=(jax.ShapeDtypeStruct(adjoint_in.shape,...  62.8 us
    pallas_call x1, Pallas kernels, body(): pl.pallas_call(hand_over, out_shape=(jax.ShapeDtypeStruct(adjoint_in.shap...  2.05 us

profile of v4, /device:TPU:1, one launch (start us, length us, event | category | flops | bytes accessed | tf_op | source)
XLA Modules:
  0.0 65.5 jit_solution(4960490350935675006)
XLA Ops:
  0.6 62.8 %shard_map.104 = (f32[4,48,8,128]{3,2,1,0:T(8,128)}, f32[48,8,128]{2,1,0:T(8,128)}) custom-call(f32[4,48,8,128]{3,2,1,0:T(8,128)} %adj_h.1, f32[4,48,8,128]{3,2,1,0:T(8,128)} %conc_h.1, f32[48,8,128]{2,1,0:T(8,128)} %press_h.1, f32[48,8,128]{2,1,0:T(8,128)} %perm_h.1, f32[48,8,128]{2,1,0:T(8,128)} %por_h.1, f32[48,8,128]{2,1,0:T(8,128)} %sto_h.1, ...), custom_call_target="tpu_custom_call" | custom-call | tf_op jit(solution)/shard_map/pallas_call | solution.py:653
  63.4 2.0 %shard_map.105 = (f32[4,48,8,128]{3,2,1,0:T(8,128)}, f32[48,8,128]{2,1,0:T(8,128)}) custom-call(f32[4,48,8,128]{3,2,1,0:T(8,128)} %get-tuple-element.4.adj, f32[48,8,128]{2,1,0:T(8,128)} %get-tuple-element.5.grad), custom_call_target="tpu_custom_call" | custom-call | tf_op jit(solution)/shard_map/pallas_call | solution.py:703
